TPU v7x, 256 devices: a whole 4x4x8 slice. The times are simulated.
256 devices in a mesh: tilt: 8 (over z), tile: 32 (over x, y, core).
Axes of the slice: x: 4, y: 4, z: 8, core: 2. Of those that a mesh axis runs over, the one named last changes fastest.
Arguments:
- volumes: bfloat16 [192, 128, 64, 128], P('tile', 'tilt'), may hold values from -0.75 to 0.75
- angles: float32 [16], replicated, may hold values from -1.05 to 1.05
- defocus: float32 [16], P('tilt'), may hold values from 0.01 to 0.1
- row_offsets: int32 [192, 16], P('tile', 'tilt'), may hold values from 0 to 4095, as said below
- col_offsets: int32 [192, 16], P('tile', 'tilt'), may hold values from 0 to 128
- measured: float32 [16, 4096, 256], P('tilt', 'tile'), may hold values from -6 to 6
Outputs:
- residual: float32 [16, 4096, 256], P('tilt', 'tile')
- volume_step: float32 [192, 128, 64, 128], P('tile', 'tilt')
Inputs may be any that keep to these rules, and one draw needn't show every extreme that they name: row_offsets[b, t] // 128 is the strip that holds the window's top row. Among the 6 boxes of one index of tile and the 2 tilts of one index of tilt, at most 2 windows have their top row in the same strip; in every draw, for every index of tilt, one strip receives exactly 2 such windows from every index of tile.
All inputs are finite; a program needn't handle non-finite values.
Results may differ from a plain program's by a relative error of at most 0.0047.
Values may be sent and summed in bfloat16 or wider, within the bound.
A program may use at most 64 MiB of HBM per device.

v0:
```python
import jax
import jax.numpy as jnp
from jax import lax
from jax.sharding import PartitionSpec as P

HR = 8


def from_behind(block, axis, distance):
    devices = range(lax.axis_size(axis))
    route = [(i - distance, i) for i in devices if i - distance in devices]
    return lax.ppermute(block, axis, route)


def extended_2(x, sides, width):
    for axis, dim in sides:
        devices, length = (lax.axis_size(axis), x.shape[dim])
        up = [(i, (i + 1) % devices) for i in range(devices - 1)]
        down = [(j, i) for i, j in up]
        last = lax.slice_in_dim(x, length - width, length, axis=dim)
        leading = lax.slice_in_dim(x, 0, width, axis=dim)
        before = lax.ppermute(last, axis, up)
        after = lax.ppermute(leading, axis, down)
        x = jnp.concatenate([before, x, after], axis=dim)
    return x


def shear_shift(tilt_angle, depth_values, box_depth):
    return (depth_values - (box_depth - 1) / 2.0) * jnp.sin(tilt_angle)


def tap_weight(offset, layer_shift):
    return jnp.maximum(0.0, 1.0 - jnp.abs(offset - layer_shift))


def point_spread(rho_sq, defocus, radius):
    spread_scale = float(radius * radius)
    return jnp.exp(-rho_sq / (2.0 * spread_scale)) * jnp.cos(defocus * rho_sq) / spread_scale


def shear_table(tilt_angle, depth_values, box_depth, box_width):
    across = jnp.arange(box_width, dtype=jnp.float32)
    offsets = across[None, :] - across[:, None]
    weights = tap_weight(
        offsets[None, :, :], shear_shift(tilt_angle, depth_values, box_depth)[:, None, None]
    )
    return weights.reshape(depth_values.shape[0] * box_width, box_width).astype(jnp.bfloat16)


def transfer_matrix(defocus, radius, block_width):
    kernel_reach = 2 * radius + 1
    row_index = jnp.arange(kernel_reach, dtype=jnp.int32) - radius
    column_index = jnp.arange(block_width + 2 * radius, dtype=jnp.int32)
    output_index = jnp.arange(block_width, dtype=jnp.int32)
    column_apart = column_index[:, None] - radius - output_index[None, :]
    rho_sq = (row_index[:, None, None] ** 2 + column_apart[None] ** 2).astype(jnp.float32)
    values = point_spread(rho_sq[None], defocus[:, None, None, None], radius)
    inside = (jnp.abs(column_apart) <= radius)[None, None]
    kernel_table = jnp.where(inside, values, 0.0)
    return kernel_table.reshape(
        defocus.shape[0], kernel_reach * (block_width + 2 * radius), block_width
    ).astype(jnp.bfloat16)


def convolve(rimmed, kernel, radius, block_width):
    height = rimmed.shape[1] - 2 * radius
    image_width = rimmed.shape[2]
    padded = jnp.pad(rimmed, ((0, 0), (0, 0), (radius, radius)))
    results = []
    for column_start in range(0, image_width, block_width):
        stacked = jnp.concatenate(
            [
                padded[
                    :,
                    offset_row : offset_row + height,
                    column_start : column_start + block_width + 2 * radius,
                ]
                for offset_row in range(2 * radius + 1)
            ],
            axis=2,
        )
        results.append(
            jnp.einsum("tra,tao->tro", stacked, kernel, preferred_element_type=jnp.float32)
        )
    return jnp.concatenate(results, axis=2)


def column_table(start_columns, breadth, image_width):
    image_columns = jnp.arange(image_width, dtype=jnp.int32)[None, None, :]
    window_columns = (
        start_columns[:, None, None] + jnp.arange(breadth, dtype=jnp.int32)[None, :, None]
    )
    return (image_columns == window_columns).astype(jnp.bfloat16)


def place_windows(canvas, windows, meta, base_row):
    tilt_count, canvas_rows, image_width = canvas.shape
    slot_total, height, breadth = windows.shape
    placed = jnp.einsum(
        "syx,sxc->syc",
        windows,
        column_table(meta[:, 2], breadth, image_width),
        preferred_element_type=jnp.float32,
    )
    placed = placed.astype(jnp.bfloat16).reshape(slot_total * height, image_width)
    target_rows = (
        meta[:, 0][:, None] * canvas_rows
        + base_row
        + meta[:, 1][:, None]
        + jnp.arange(height, dtype=jnp.int32)[None, :]
    )
    row_onehot = (
        jnp.arange(tilt_count * canvas_rows, dtype=jnp.int32)[:, None]
        == target_rows.reshape(slot_total * height)[None, :]
    ).astype(jnp.bfloat16)
    added = jnp.dot(row_onehot, placed, preferred_element_type=jnp.float32)
    return added.reshape(tilt_count, canvas_rows, image_width)


def cut_windows(extended, meta, base_row, height, breadth):
    image_width = extended.shape[2]

    def one_slot(slot_entry):
        return lax.dynamic_slice(
            extended, (slot_entry[0], base_row + slot_entry[1], 0), (1, height, image_width)
        )[0]

    full_rows = jax.vmap(one_slot)(meta)
    picked = jnp.einsum(
        "syc,sxc->syx",
        full_rows,
        column_table(meta[:, 2], breadth, image_width),
        preferred_element_type=jnp.float32,
    )
    return picked.astype(jnp.bfloat16)


def shards(volumes, angles, defocus, row_offsets, col_offsets, measured):
    box_count, slab_rows, box_depth, box_width = volumes.shape
    tilt_count, strip_rows, image_width = measured.shape
    tile_count = lax.axis_size("tile")
    group_count = lax.axis_size("tilt")
    box_height = slab_rows * group_count
    item_count = box_count * tilt_count
    capacity = max(2, (item_count + tile_count - 1) // tile_count)
    slot_count = tile_count * capacity
    block_width = min(128, image_width)
    depth_values = jnp.arange(box_depth, dtype=jnp.float32)
    grouped_angles = angles.reshape(group_count, tilt_count)
    flattened = volumes.reshape(box_count, slab_rows, box_depth * box_width)

    def build_tables(some_angles):
        return jax.vmap(
            lambda tilt_angle: shear_table(tilt_angle, depth_values, box_depth, box_width)
        )(some_angles)

    def project_group(group_angles):
        return jnp.einsum(
            "byq,tqo->tbyo",
            flattened,
            build_tables(group_angles),
            preferred_element_type=jnp.float32,
        ).astype(jnp.bfloat16)

    slab_projections = lax.map(project_group, grouped_angles).reshape(
        tilt_count * group_count, box_count, slab_rows, box_width
    )
    windows = lax.all_to_all(slab_projections, "tilt", split_axis=0, concat_axis=2, tiled=True)
    item_rows = row_offsets.T.reshape(item_count)
    item_columns = col_offsets.T.reshape(item_count)
    target = item_rows // strip_rows
    within = item_rows - target * strip_rows
    item_tilt = jnp.arange(item_count, dtype=jnp.int32) // box_count
    same_target = target[:, None] == target[None, :]
    earlier = (
        jnp.arange(item_count, dtype=jnp.int32)[None, :]
        < jnp.arange(item_count, dtype=jnp.int32)[:, None]
    )
    ranking = jnp.sum((same_target & earlier).astype(jnp.int32), axis=1)
    slot_of = target * capacity + ranking
    routing = jnp.arange(slot_count, dtype=jnp.int32)[:, None] == slot_of[None, :]
    send_home = jnp.dot(
        routing.astype(jnp.bfloat16),
        windows.reshape(item_count, box_height * box_width),
        preferred_element_type=jnp.float32,
    )
    send_home = send_home.astype(jnp.bfloat16).reshape(slot_count, box_height, box_width)
    item_meta = jnp.stack([item_tilt, within, item_columns], axis=1)
    meta_home = jnp.sum(routing.astype(jnp.int32)[:, :, None] * item_meta[None], axis=1)
    canvas = jnp.zeros((tilt_count, 2 * strip_rows + box_height, image_width), jnp.float32)
    got_home, seen_home = (
        lax.all_to_all(send_home, "tile", split_axis=0, concat_axis=0, tiled=True),
        lax.all_to_all(meta_home, "tile", split_axis=0, concat_axis=0, tiled=True),
    )
    canvas = place_windows(canvas, got_home, seen_home, strip_rows)
    overhang = from_behind(canvas[:, 2 * strip_rows :], "tile", 1)
    predicted = canvas[:, strip_rows : 2 * strip_rows].at[:, :box_height].add(overhang)
    kernel = transfer_matrix(defocus, HR, block_width)
    rimmed = extended_2(predicted.astype(jnp.bfloat16), (("tile", 1),), HR)
    residual = measured - convolve(rimmed, kernel, HR, block_width)
    residual_edges = extended_2(residual.astype(jnp.bfloat16), (("tile", 1),), HR)
    back_half = convolve(residual_edges, kernel, HR, block_width).astype(jnp.bfloat16)
    blank_rows = jnp.zeros((tilt_count, strip_rows, image_width), jnp.bfloat16)
    next_rows = from_behind(back_half, "tile", -1)
    extended = jnp.concatenate([blank_rows, back_half, next_rows], axis=1)
    cut_home = cut_windows(extended, seen_home, strip_rows, box_height, box_width)
    back_slots = lax.all_to_all(cut_home, "tile", split_axis=0, concat_axis=0, tiled=True)
    back_items = jnp.dot(
        routing.T.astype(jnp.bfloat16),
        back_slots.reshape(slot_count, box_height * box_width),
        preferred_element_type=jnp.float32,
    )
    back_items = back_items.astype(jnp.bfloat16).reshape(
        tilt_count, box_count, box_height, box_width
    )
    scale_factor = 1.0 / (tilt_count * group_count)
    initial = jnp.zeros((box_count, slab_rows, box_depth * box_width), jnp.float32)
    back_rows = lax.all_to_all(back_items, "tilt", split_axis=2, concat_axis=0, tiled=True)
    grouped_rows = back_rows.reshape(group_count, tilt_count, box_count, slab_rows, box_width)

    def add_group(summed, inputs):
        group_windows, group_angles = inputs
        return (
            summed
            + jnp.einsum(
                "tbyo,tqo->byq",
                group_windows,
                build_tables(group_angles),
                preferred_element_type=jnp.float32,
            ),
            None,
        )

    summed, _ = lax.scan(add_group, initial, (grouped_rows, grouped_angles))
    volume_step = (summed * scale_factor).reshape(box_count, slab_rows, box_depth, box_width)
    return (residual, volume_step)


def solution(mesh):
    in_specs = (
        P("tile", "tilt", None, None),
        P(),
        P("tilt"),
        P("tile", "tilt"),
        P("tile", "tilt"),
        P("tilt", "tile", None),
    )
    out_specs = (P("tilt", "tile", None), P("tile", "tilt", None, None))
    return jax.shard_map(shards, mesh=mesh, in_specs=in_specs, out_specs=out_specs, check_vma=False)
```

profile of v0, /device:TPU:2, one launch (start us, length us, event | category | flops | bytes accessed | tf_op | source)
XLA Modules:
  0.0 284.4 jit_solution(13812538858229623420)
XLA Ops:
  0.6 0.7 reshape.520
  1.4 2.6 reshape.521
  4.0 31.0 %while.28 = (s32[]{:T(128)}, bf16[8,2,6,16,128]{4,3,2,1,0:T(8,128)(2,1)}, f32[8,2]{1,0:T(8,128)S(1)}, bf16[6,16,8192]{2,1,0:T(8,128)(2,1)S(1)}, s32[]{:T(128)}) while((s32[]{:T(128)}, bf16[8,2,6,16,128]{4,3,2,1,0:T(8,128)(2,1)}, f32[8,2]{1,0:T(8,128)S(1)}, bf16[6,16,8192]{2,1,0:T(8,128)(2,1)S(1)}, s32[]{:T(128)}) %tuple.131), condition=%wide.region_3.4_spmd.clone, body=%wide.region_2.3_spmd.clone.sunk | while | flops 413180096 | bytes 10405977 | solution.py:165
  4.8 3.1 %fusion.104 = bf16[8,2,6,16,128]{4,3,2,1,0:T(8,128)(2,1)} fusion(bf16[8,2,6,16,128]{4,3,2,1,0:T(8,128)(2,1)} %get-tuple-element.364, s32[]{:T(128)} %get-tuple-element.363, bf16[6,16,8192]{2,1,0:T(8,128)(2,1)S(1)} %get-tuple-element.371, f32[2,8192]{1,0:T(2,128)S(1)} %bitcast.148, f32[8192,128]{1,0:T(8,128)S(1)} %bitcast.140), kind=kOutput, calls=%fused_computation.9.clone.1 | convolution fusion | flops 413163520 | bytes 5882368 | tf_op jit(solution)/shard_map/while/body/eval_jaxpr/byq,tqo->tbyo/dot_general | solution.py:158
  8.6 3.1 %fusion.104 = bf16[8,2,6,16,128]{4,3,2,1,0:T(8,128)(2,1)} fusion(bf16[8,2,6,16,128]{4,3,2,1,0:T(8,128)(2,1)} %get-tuple-element.364, s32[]{:T(128)} %get-tuple-element.363, bf16[6,16,8192]{2,1,0:T(8,128)(2,1)S(1)} %get-tuple-element.371, f32[2,8192]{1,0:T(2,128)S(1)} %bitcast.148, f32[8192,128]{1,0:T(8,128)S(1)} %bitcast.140), kind=kOutput, calls=%fused_computation.9.clone.1 | convolution fusion | flops 413163520 | bytes 5882368 | tf_op jit(solution)/shard_map/while/body/eval_jaxpr/byq,tqo->tbyo/dot_general | solution.py:158
  12.0 0.5 sub.331
  12.5 3.1 %fusion.104 = bf16[8,2,6,16,128]{4,3,2,1,0:T(8,128)(2,1)} fusion(bf16[8,2,6,16,128]{4,3,2,1,0:T(8,128)(2,1)} %get-tuple-element.364, s32[]{:T(128)} %get-tuple-element.363, bf16[6,16,8192]{2,1,0:T(8,128)(2,1)S(1)} %get-tuple-element.371, f32[2,8192]{1,0:T(2,128)S(1)} %bitcast.148, f32[8192,128]{1,0:T(8,128)S(1)} %bitcast.140), kind=kOutput, calls=%fused_computation.9.clone.1 | convolution fusion | flops 413163520 | bytes 5882368 | tf_op jit(solution)/shard_map/while/body/eval_jaxpr/byq,tqo->tbyo/dot_general | solution.py:158
  15.9 0.5 sub.331
  16.4 3.1 %fusion.104 = bf16[8,2,6,16,128]{4,3,2,1,0:T(8,128)(2,1)} fusion(bf16[8,2,6,16,128]{4,3,2,1,0:T(8,128)(2,1)} %get-tuple-element.364, s32[]{:T(128)} %get-tuple-element.363, bf16[6,16,8192]{2,1,0:T(8,128)(2,1)S(1)} %get-tuple-element.371, f32[2,8192]{1,0:T(2,128)S(1)} %bitcast.148, f32[8192,128]{1,0:T(8,128)S(1)} %bitcast.140), kind=kOutput, calls=%fused_computation.9.clone.1 | convolution fusion | flops 413163520 | bytes 5882368 | tf_op jit(solution)/shard_map/while/body/eval_jaxpr/byq,tqo->tbyo/dot_general | solution.py:158
  20.3 3.1 %fusion.104 = bf16[8,2,6,16,128]{4,3,2,1,0:T(8,128)(2,1)} fusion(bf16[8,2,6,16,128]{4,3,2,1,0:T(8,128)(2,1)} %get-tuple-element.364, s32[]{:T(128)} %get-tuple-element.363, bf16[6,16,8192]{2,1,0:T(8,128)(2,1)S(1)} %get-tuple-element.371, f32[2,8192]{1,0:T(2,128)S(1)} %bitcast.148, f32[8192,128]{1,0:T(8,128)S(1)} %bitcast.140), kind=kOutput, calls=%fused_computation.9.clone.1 | convolution fusion | flops 413163520 | bytes 5882368 | tf_op jit(solution)/shard_map/while/body/eval_jaxpr/byq,tqo->tbyo/dot_general | solution.py:158
  24.1 3.1 %fusion.104 = bf16[8,2,6,16,128]{4,3,2,1,0:T(8,128)(2,1)} fusion(bf16[8,2,6,16,128]{4,3,2,1,0:T(8,128)(2,1)} %get-tuple-element.364, s32[]{:T(128)} %get-tuple-element.363, bf16[6,16,8192]{2,1,0:T(8,128)(2,1)S(1)} %get-tuple-element.371, f32[2,8192]{1,0:T(2,128)S(1)} %bitcast.148, f32[8192,128]{1,0:T(8,128)S(1)} %bitcast.140), kind=kOutput, calls=%fused_computation.9.clone.1 | convolution fusion | flops 413163520 | bytes 5882368 | tf_op jit(solution)/shard_map/while/body/eval_jaxpr/byq,tqo->tbyo/dot_general | solution.py:158
  28.0 3.1 %fusion.104 = bf16[8,2,6,16,128]{4,3,2,1,0:T(8,128)(2,1)} fusion(bf16[8,2,6,16,128]{4,3,2,1,0:T(8,128)(2,1)} %get-tuple-element.364, s32[]{:T(128)} %get-tuple-element.363, bf16[6,16,8192]{2,1,0:T(8,128)(2,1)S(1)} %get-tuple-element.371, f32[2,8192]{1,0:T(2,128)S(1)} %bitcast.148, f32[8192,128]{1,0:T(8,128)S(1)} %bitcast.140), kind=kOutput, calls=%fused_computation.9.clone.1 | convolution fusion | flops 413163520 | bytes 5882368 | tf_op jit(solution)/shard_map/while/body/eval_jaxpr/byq,tqo->tbyo/dot_general | solution.py:158
  31.9 3.1 %fusion.104 = bf16[8,2,6,16,128]{4,3,2,1,0:T(8,128)(2,1)} fusion(bf16[8,2,6,16,128]{4,3,2,1,0:T(8,128)(2,1)} %get-tuple-element.364, s32[]{:T(128)} %get-tuple-element.363, bf16[6,16,8192]{2,1,0:T(8,128)(2,1)S(1)} %get-tuple-element.371, f32[2,8192]{1,0:T(2,128)S(1)} %bitcast.148, f32[8192,128]{1,0:T(8,128)S(1)} %bitcast.140), kind=kOutput, calls=%fused_computation.9.clone.1 | convolution fusion | flops 413163520 | bytes 5882368 | tf_op jit(solution)/shard_map/while/body/eval_jaxpr/byq,tqo->tbyo/dot_general | solution.py:158
  35.0 8.5 %all-to-all-start.1 = ((bf16[16,6,16,128]{3,2,1,0:T(8,128)(2,1)}), bf16[16,6,16,128]{3,2,1,0:T(8,128)(2,1)S(1)}, u32[]{:S(2)}, u32[]{:S(2)}) async-start(bf16[16,6,16,128]{3,2,1,0:T(8,128)(2,1)} %bitcast.6), calls=%async_computation.1 | async-start | bytes 786432 | tf_op jit(solution)/shard_map/all_to_all | solution.py:168
  44.1 0.7 copy.74
  44.8 13.3 %all-to-all-done.1 = bf16[16,6,16,128]{3,2,1,0:T(8,128)(2,1)S(1)} async-done(((bf16[16,6,16,128]{3,2,1,0:T(8,128)(2,1)}), bf16[16,6,16,128]{3,2,1,0:T(8,128)(2,1)S(1)}, u32[]{:S(2)}, u32[]{:S(2)}) %all-to-all-start.1) | async-done | bytes 393248 | tf_op jit(solution)/shard_map/all_to_all | solution.py:168
  58.1 7.6 %all-to-all-start = ((s32[32,2,3]{2,1,0:T(2,128)}), s32[32,2,3]{2,1,0:T(2,128)S(1)}, u32[]{:S(2)}, u32[]{:S(2)}) async-start(s32[32,2,3]{2,1,0:T(2,128)} %bitcast.2), calls=%async_computation | async-start | bytes 65536 | tf_op jit(solution)/shard_map/all_to_all | solution.py:193
  66.0 0.8 fusion.51
  66.9 1.9 copy.82
  68.8 3.2 %all-to-all-done = s32[32,2,3]{2,1,0:T(2,128)S(1)} async-done(((s32[32,2,3]{2,1,0:T(2,128)}), s32[32,2,3]{2,1,0:T(2,128)S(1)}, u32[]{:S(2)}, u32[]{:S(2)}) %all-to-all-start) | async-done | bytes 800 | tf_op jit(solution)/shard_map/all_to_all | solution.py:193
  72.0 5.1 %all-to-all-start.2 = ((bf16[64,128,128]{2,1,0:T(8,128)(2,1)}), bf16[64,128,128]{2,1,0:T(8,128)(2,1)S(1)}, u32[]{:S(2)}, u32[]{:S(2)}) async-start(bf16[64,128,128]{2,1,0:T(8,128)(2,1)} %bitcast.142), calls=%async_computation.2 | async-start | bytes 4194304 | tf_op jit(solution)/shard_map/all_to_all | solution.py:192
  77.7 25.4 %all-to-all-done.2 = bf16[64,128,128]{2,1,0:T(8,128)(2,1)S(1)} async-done(((bf16[64,128,128]{2,1,0:T(8,128)(2,1)}), bf16[64,128,128]{2,1,0:T(8,128)(2,1)S(1)}, u32[]{:S(2)}, u32[]{:S(2)}) %all-to-all-start.2) | async-done | bytes 2097184 | tf_op jit(solution)/shard_map/all_to_all | solution.py:192
  103.1 2.4 fusion.45
  105.5 3.5 %fusion.36 = f32[2,384,256]{2,1,0:T(8,128)S(1)} fusion(bf16[8192,256,1]{1,0,2:T(8,128)(2,1)S(1)} %bitcast.144, s32[8192]{0:T(1024)S(1)} %add_bitcast_fusion, s32[2,384]{1,0:T(2,128)S(1)} %multiply_add_fusion), kind=kOutput, calls=%fused_computation.38 | convolution fusion | flops 3227516928 | bytes 5016576 | tf_op jit(solution)/shard_map/dot_general | solution.py:116
  109.0 2.3 collective-permute-start
  112.4 6.4 %collective-permute-done = f32[2,128,256]{2,1,0:T(8,128)S(1)} collective-permute-done((f32[2,128,256]{2,1,0:T(8,128)S(1)}, f32[2,128,256]{2,1,0:T(8,128)S(1)}, u32[]{:S(2)}, u32[]{:S(2)}) %collective-permute-start) | collective-permute-done | bytes 262176 | tf_op jit(solution)/shard_map/ppermute | solution.py:12
  118.9 1.9 collective-permute-start.1
  120.8 5.9 %collective-permute-start.2 = (bf16[2,8,256]{2,1,0:T(8,128)(2,1)S(1)}, bf16[2,8,256]{2,1,0:T(8,128)(2,1)S(1)}, u32[]{:S(2)}, u32[]{:S(2)}) collective-permute-start(bf16[2,8,256]{2,1,0:T(8,128)(2,1)S(1)} %get-tuple-element.300), channel_id=1, source_target_pairs={{1,0},{2,1},{3,2},{4,3},{5,4},{6,5},{7,6},{8,7},{9,8},{10,9},{11,1... | collective-permute-start | bytes 24584 | tf_op jit(solution)/shard_map/ppermute | solution.py:23
  126.8 8.9 %select_convert_fusion = bf16[2,2448,128]{2,1,0:T(8,128)(2,1)S(1)} fusion(f32[2448,128]{1,0:T(8,128)S(1)} %fusion.52, f32[2]{0:T(128)S(1)} %copy-done.2, f32[2448,128]{1,0:T(8,128)S(1)} %multiply_exponential_fusion, pred[2448,128]{1,0:T(8,128)(4,1)S(1)} %bitcast.152), kind=kLoop, calls=%fused_computation.51 | loop fusion | flops 3133440 | bytes 4073480 | tf_op jit(solution)/shard_map/convert_element_type | solution.py:62
  136.0 1.3 fusion.77
  137.3 1.3 fusion.78
  138.6 2.9 %concatenate.34 = bf16[2,128,2448]{2,1,0:T(8,128)(2,1)S(1)} concatenate(bf16[2,128,144]{2,1,0:T(8,128)(2,1)} %get-tuple-element.295, bf16[2,128,144]{2,1,0:T(8,128)(2,1)} %get-tuple-element.294, bf16[2,128,144]{2,1,0:T(8,128)(2,1)} %get-tuple-element.293, bf16[2,128,144]{2,1,0:T(8,128)(2,1)} %get-tuple-element.292, bf16[2,128,144]{2,1,0:T(8,128)(2,1)} %get-tuple-element.291, ...), dimensions={2} | concatenate | bytes 2506752 | tf_op jit(solution)/shard_map/concatenate | solution.py:71
  141.6 1.3 fusion.82
  142.8 2.8 concatenate.35
  145.6 0.6 fusion.83
  146.5 0.8 fusion.76
  147.4 1.9 collective-permute-start.3
  149.3 5.8 %collective-permute-start.4 = (bf16[2,8,256]{1,2,0:T(8,128)(2,1)S(1)}, bf16[2,8,256]{1,2,0:T(8,128)(2,1)S(1)}, u32[]{:S(2)}, u32[]{:S(2)}) collective-permute-start(bf16[2,8,256]{1,2,0:T(8,128)(2,1)S(1)} %get-tuple-element.298), channel_id=1, source_target_pairs={{1,0},{2,1},{3,2},{4,3},{5,4},{6,5},{7,6},{8,7},{9,8},{10,9},{11,1... | collective-permute-start | bytes 24584 | tf_op jit(solution)/shard_map/ppermute | solution.py:23
  155.1 0.7 collective-permute-done.3
  155.8 1.8 collective-permute-done.4
  160.0 0.6 convolution_convert_fusion.3
  160.7 0.6 convolution_convert_fusion.2
  161.3 6.1 %collective-permute-start.5 = (bf16[2,128,256]{1,2,0:T(8,128)(2,1)S(1)}, bf16[2,128,256]{1,2,0:T(8,128)(2,1)S(1)}, u32[]{:S(2)}, u32[]{:S(2)}) collective-permute-start(bf16[2,128,256]{1,2,0:T(8,128)(2,1)S(1)} %pad_maximum_fusion.1), channel_id=1, source_target_pairs={{1,0},{2,1},{3,2},{4,3},{5,4},{6,5},{7,6},{8,7},{9,8},{10,9},{11,1... | collective-permute-start | bytes 393224 | tf_op jit(solution)/shard_map/ppermute | solution.py:12
  167.4 2.3 collective-permute-done.5
  169.8 0.6 copy.64
  170.4 9.2 %gather_fusion = bf16[64,128,256]{2,0,1:T(8,128)(2,1)} fusion(bf16[2,384,256]{2,0,1:T(2,128)(2,1)S(1)} %copy.64, s32[64]{0:T(128)S(1)} %get-tuple-element.304), kind=kCustom, calls=%fused_computation | custom fusion | bytes 8389376 | tf_op jit(solution)/shard_map/vmap()/gather | solution.py:124
  179.7 5.3 %fusion.48 = bf16[64,128,128]{2,1,0:T(8,128)(2,1)S(1)} fusion(s32[64,128]{1,0:T(8,128)S(1)} %iota_add_fusion.2, bf16[64,128,256]{2,0,1:T(8,128)(2,1)} %gather_fusion), kind=kOutput, calls=%fused_computation.54 | convolution fusion | flops 540016640 | bytes 6324224 | tf_op jit(solution)/shard_map/syc,sxc->syx/dot_general | solution.py:129
  185.0 34.1 %all_to_all.52 = bf16[64,128,128]{2,1,0:T(8,128)(2,1)S(1)} all-to-all(bf16[64,128,128]{2,1,0:T(8,128)(2,1)S(1)} %fusion.48), channel_id=1, replica_groups=mesh['tilt'=8,'tile'=32] {'tile'}, dimensions={0} | all-to-all | bytes 4194304 | tf_op jit(solution)/shard_map/all_to_all | solution.py:207
  219.0 1.2 convolution_convert_fusion.1
  220.4 1.2 copy.66
  221.6 3.7 %all-to-all-start.4 = ((bf16[2,6,128,128]{3,0,1,2:T(2,128)(2,1)}), bf16[2,6,128,128]{3,0,1,2:T(2,128)(2,1)S(1)}, u32[]{:S(2)}, u32[]{:S(2)}) async-start(bf16[2,6,128,128]{3,0,1,2:T(2,128)(2,1)} %copy.66), calls=%async_computation.4 | async-start | bytes 786432 | tf_op jit(solution)/shard_map/all_to_all | solution.py:218
  225.3 1.8 copy.69
  227.1 13.9 %all-to-all-done.4 = bf16[2,6,128,128]{3,0,1,2:T(2,128)(2,1)S(1)} async-done(((bf16[2,6,128,128]{3,0,1,2:T(2,128)(2,1)}), bf16[2,6,128,128]{3,0,1,2:T(2,128)(2,1)S(1)}, u32[]{:S(2)}, u32[]{:S(2)}) %all-to-all-start.4) | async-done | bytes 393248 | tf_op jit(solution)/shard_map/all_to_all | solution.py:218
  241.0 0.8 copy.67
  241.8 40.1 %while.29 = (s32[]{:T(128)}, f32[6,16,8192]{2,1,0:T(8,128)S(1)}, bf16[8,2,6,16,128]{4,3,0,2,1:T(8,128)(2,1)}, f32[8,2]{1,0:T(8,128)S(1)}, s32[]{:T(128)}, /*index=5*/s32[]{:T(128)}) while((s32[]{:T(128)}, f32[6,16,8192]{2,1,0:T(8,128)S(1)}, bf16[8,2,6,16,128]{4,3,0,2,1:T(8,128)(2,1)}, f32[8,2]{1,0:T(8,128)S(1)}, s32[]{:T(128)}, ...), condition=%wide.region_5.6_spmd.clone, body=%wide.region_4.5_spmd.clone.sunk | while | flops 414728384 | bytes 15124587 | solution.py:234
  242.6 4.2 %fusion.106 = f32[6,16,8192]{2,1,0:T(8,128)S(1)} fusion(f32[2,8192]{1,0:T(2,128)S(1)} %bitcast.147, f32[8192,128]{1,0:T(8,128)S(1)} %bitcast.139, f32[6,16,8192]{2,1,0:T(8,128)S(1)} %get-tuple-element.380, pred[]{:T(512)S(6)} %compare.118, bf16[8,2,6,16,128]{4,3,0,2,1:T(8,128)(2,1)} %get-tuple-element.387, s32[]{:T(128)} %get-tuple-element.379), kind=kOutput, calls=%fused_computation.21.clone.1 | convolution fusion | flops 414711808 | bytes 10600961 | tf_op jit(solution)/shard_map/while/body/eval_jaxpr/tbyo,tqo->byq/dot_general | solution.py:225
  247.7 4.2 %fusion.106 = f32[6,16,8192]{2,1,0:T(8,128)S(1)} fusion(f32[2,8192]{1,0:T(2,128)S(1)} %bitcast.147, f32[8192,128]{1,0:T(8,128)S(1)} %bitcast.139, f32[6,16,8192]{2,1,0:T(8,128)S(1)} %get-tuple-element.380, pred[]{:T(512)S(6)} %compare.118, bf16[8,2,6,16,128]{4,3,0,2,1:T(8,128)(2,1)} %get-tuple-element.387, s32[]{:T(128)} %get-tuple-element.379), kind=kOutput, calls=%fused_computation.21.clone.1 | convolution fusion | flops 414711808 | bytes 10600961 | tf_op jit(solution)/shard_map/while/body/eval_jaxpr/tbyo,tqo->byq/dot_general | solution.py:225
  252.7 4.2 %fusion.106 = f32[6,16,8192]{2,1,0:T(8,128)S(1)} fusion(f32[2,8192]{1,0:T(2,128)S(1)} %bitcast.147, f32[8192,128]{1,0:T(8,128)S(1)} %bitcast.139, f32[6,16,8192]{2,1,0:T(8,128)S(1)} %get-tuple-element.380, pred[]{:T(512)S(6)} %compare.118, bf16[8,2,6,16,128]{4,3,0,2,1:T(8,128)(2,1)} %get-tuple-element.387, s32[]{:T(128)} %get-tuple-element.379), kind=kOutput, calls=%fused_computation.21.clone.1 | convolution fusion | flops 414711808 | bytes 10600961 | tf_op jit(solution)/shard_map/while/body/eval_jaxpr/tbyo,tqo->byq/dot_general | solution.py:225
  257.7 4.2 %fusion.106 = f32[6,16,8192]{2,1,0:T(8,128)S(1)} fusion(f32[2,8192]{1,0:T(2,128)S(1)} %bitcast.147, f32[8192,128]{1,0:T(8,128)S(1)} %bitcast.139, f32[6,16,8192]{2,1,0:T(8,128)S(1)} %get-tuple-element.380, pred[]{:T(512)S(6)} %compare.118, bf16[8,2,6,16,128]{4,3,0,2,1:T(8,128)(2,1)} %get-tuple-element.387, s32[]{:T(128)} %get-tuple-element.379), kind=kOutput, calls=%fused_computation.21.clone.1 | convolution fusion | flops 414711808 | bytes 10600961 | tf_op jit(solution)/shard_map/while/body/eval_jaxpr/tbyo,tqo->byq/dot_general | solution.py:225
  262.7 4.2 %fusion.106 = f32[6,16,8192]{2,1,0:T(8,128)S(1)} fusion(f32[2,8192]{1,0:T(2,128)S(1)} %bitcast.147, f32[8192,128]{1,0:T(8,128)S(1)} %bitcast.139, f32[6,16,8192]{2,1,0:T(8,128)S(1)} %get-tuple-element.380, pred[]{:T(512)S(6)} %compare.118, bf16[8,2,6,16,128]{4,3,0,2,1:T(8,128)(2,1)} %get-tuple-element.387, s32[]{:T(128)} %get-tuple-element.379), kind=kOutput, calls=%fused_computation.21.clone.1 | convolution fusion | flops 414711808 | bytes 10600961 | tf_op jit(solution)/shard_map/while/body/eval_jaxpr/tbyo,tqo->byq/dot_general | solution.py:225
  267.7 4.2 %fusion.106 = f32[6,16,8192]{2,1,0:T(8,128)S(1)} fusion(f32[2,8192]{1,0:T(2,128)S(1)} %bitcast.147, f32[8192,128]{1,0:T(8,128)S(1)} %bitcast.139, f32[6,16,8192]{2,1,0:T(8,128)S(1)} %get-tuple-element.380, pred[]{:T(512)S(6)} %compare.118, bf16[8,2,6,16,128]{4,3,0,2,1:T(8,128)(2,1)} %get-tuple-element.387, s32[]{:T(128)} %get-tuple-element.379), kind=kOutput, calls=%fused_computation.21.clone.1 | convolution fusion | flops 414711808 | bytes 10600961 | tf_op jit(solution)/shard_map/while/body/eval_jaxpr/tbyo,tqo->byq/dot_general | solution.py:225
  272.7 4.2 %fusion.106 = f32[6,16,8192]{2,1,0:T(8,128)S(1)} fusion(f32[2,8192]{1,0:T(2,128)S(1)} %bitcast.147, f32[8192,128]{1,0:T(8,128)S(1)} %bitcast.139, f32[6,16,8192]{2,1,0:T(8,128)S(1)} %get-tuple-element.380, pred[]{:T(512)S(6)} %compare.118, bf16[8,2,6,16,128]{4,3,0,2,1:T(8,128)(2,1)} %get-tuple-element.387, s32[]{:T(128)} %get-tuple-element.379), kind=kOutput, calls=%fused_computation.21.clone.1 | convolution fusion | flops 414711808 | bytes 10600961 | tf_op jit(solution)/shard_map/while/body/eval_jaxpr/tbyo,tqo->byq/dot_general | solution.py:225
  277.8 4.2 %fusion.106 = f32[6,16,8192]{2,1,0:T(8,128)S(1)} fusion(f32[2,8192]{1,0:T(2,128)S(1)} %bitcast.147, f32[8192,128]{1,0:T(8,128)S(1)} %bitcast.139, f32[6,16,8192]{2,1,0:T(8,128)S(1)} %get-tuple-element.380, pred[]{:T(512)S(6)} %compare.118, bf16[8,2,6,16,128]{4,3,0,2,1:T(8,128)(2,1)} %get-tuple-element.387, s32[]{:T(128)} %get-tuple-element.379), kind=kOutput, calls=%fused_computation.21.clone.1 | convolution fusion | flops 414711808 | bytes 10600961 | tf_op jit(solution)/shard_map/while/body/eval_jaxpr/tbyo,tqo->byq/dot_general | solution.py:225
  282.2 2.2 copy.85
  (185 shorter events, 17.7 us)
Async XLA Ops:
  3.9 39.5 %copy-start.3 = (s32[6,2]{0,1:T(2,128)S(1)}, s32[6,2]{0,1:T(2,128)}, u32[]{:S(2)}) copy-start(s32[6,2]{0,1:T(2,128)} %param.17) | copy-start | bytes 148
  3.9 39.7 %copy-start.4 = (s32[6,2]{0,1:T(2,128)S(1)}, s32[6,2]{0,1:T(2,128)}, u32[]{:S(2)}) copy-start(s32[6,2]{0,1:T(2,128)} %param.18) | copy-start | bytes 148
  35.0 23.2 %all-to-all-start.1 = ((bf16[16,6,16,128]{3,2,1,0:T(8,128)(2,1)}), bf16[16,6,16,128]{3,2,1,0:T(8,128)(2,1)S(1)}, u32[]{:S(2)}, u32[]{:S(2)}) async-start(bf16[16,6,16,128]{3,2,1,0:T(8,128)(2,1)} %bitcast.6), calls=%async_computation.1 | async-start | bytes 786432 | tf_op jit(solution)/shard_map/all_to_all | solution.py:168
  58.1 13.9 %all-to-all-start = ((s32[32,2,3]{2,1,0:T(2,128)}), s32[32,2,3]{2,1,0:T(2,128)S(1)}, u32[]{:S(2)}, u32[]{:S(2)}) async-start(s32[32,2,3]{2,1,0:T(2,128)} %bitcast.2), calls=%async_computation | async-start | bytes 65536 | tf_op jit(solution)/shard_map/all_to_all | solution.py:193
  72.0 31.1 %all-to-all-start.2 = ((bf16[64,128,128]{2,1,0:T(8,128)(2,1)}), bf16[64,128,128]{2,1,0:T(8,128)(2,1)S(1)}, u32[]{:S(2)}, u32[]{:S(2)}) async-start(bf16[64,128,128]{2,1,0:T(8,128)(2,1)} %bitcast.142), calls=%async_computation.2 | async-start | bytes 4194304 | tf_op jit(solution)/shard_map/all_to_all | solution.py:192
  109.0 9.8 %collective-permute-start = (f32[2,128,256]{2,1,0:T(8,128)S(1)}, f32[2,128,256]{2,1,0:T(8,128)S(1)}, u32[]{:S(2)}, u32[]{:S(2)}) collective-permute-start(f32[2,128,256]{2,1,0:T(8,128)S(1)} %slice.340), channel_id=1, source_target_pairs={{0,1},{1,2},{2,3},{3,4},{4,5},{5,6},{6,7},{7,8},{8,9},{9,10},{10,1... | collective-permute-start | bytes 786440 | tf_op jit(solution)/shard_map/ppermute | solution.py:12
  111.9 14.9 %copy-start.2 = (f32[2]{0:T(128)S(1)}, f32[2]{0:T(128)}, u32[]{:S(2)}) copy-start(f32[2]{0:T(128)} %param.16) | copy-start | bytes 28
  118.9 17.0 %collective-permute-start.1 = (bf16[2,8,256]{2,1,0:T(8,128)(2,1)S(1)}, bf16[2,8,256]{2,1,0:T(8,128)(2,1)S(1)}, u32[]{:S(2)}, u32[]{:S(2)}) collective-permute-start(bf16[2,8,256]{2,1,0:T(8,128)(2,1)S(1)} %get-tuple-element.299), channel_id=1, source_target_pairs={{0,1},{1,2},{2,3},{3,4},{4,5},{5,6},{6,7},{7,8},{8,9},{9,10},{10,1... | collective-permute-start | bytes 24584 | tf_op jit(solution)/shard_map/ppermute | solution.py:22
  120.8 15.1 %collective-permute-start.2 = (bf16[2,8,256]{2,1,0:T(8,128)(2,1)S(1)}, bf16[2,8,256]{2,1,0:T(8,128)(2,1)S(1)}, u32[]{:S(2)}, u32[]{:S(2)}) collective-permute-start(bf16[2,8,256]{2,1,0:T(8,128)(2,1)S(1)} %get-tuple-element.300), channel_id=1, source_target_pairs={{1,0},{2,1},{3,2},{4,3},{5,4},{6,5},{7,6},{8,7},{9,8},{10,9},{11,1... | collective-permute-start | bytes 24584 | tf_op jit(solution)/shard_map/ppermute | solution.py:23
  126.8 8.9 %copy-start.1 = (f32[2,128,256]{2,1,0:T(8,128)S(1)}, f32[2,128,256]{2,1,0:T(8,128)}, u32[]{:S(2)}) copy-start(f32[2,128,256]{2,1,0:T(8,128)} %param.19) | copy-start | bytes 786436
  145.6 0.9 copy-start
  147.4 8.4 %collective-permute-start.3 = (bf16[2,8,256]{1,2,0:T(8,128)(2,1)S(1)}, bf16[2,8,256]{1,2,0:T(8,128)(2,1)S(1)}, u32[]{:S(2)}, u32[]{:S(2)}) collective-permute-start(bf16[2,8,256]{1,2,0:T(8,128)(2,1)S(1)} %get-tuple-element.297), channel_id=1, source_target_pairs={{0,1},{1,2},{2,3},{3,4},{4,5},{5,6},{6,7},{7,8},{8,9},{9,10},{10,1... | collective-permute-start | bytes 24584 | tf_op jit(solution)/shard_map/ppermute | solution.py:22
  149.3 8.3 %collective-permute-start.4 = (bf16[2,8,256]{1,2,0:T(8,128)(2,1)S(1)}, bf16[2,8,256]{1,2,0:T(8,128)(2,1)S(1)}, u32[]{:S(2)}, u32[]{:S(2)}) collective-permute-start(bf16[2,8,256]{1,2,0:T(8,128)(2,1)S(1)} %get-tuple-element.298), channel_id=1, source_target_pairs={{1,0},{2,1},{3,2},{4,3},{5,4},{6,5},{7,6},{8,7},{9,8},{10,9},{11,1... | collective-permute-start | bytes 24584 | tf_op jit(solution)/shard_map/ppermute | solution.py:23
  161.3 8.4 %collective-permute-start.5 = (bf16[2,128,256]{1,2,0:T(8,128)(2,1)S(1)}, bf16[2,128,256]{1,2,0:T(8,128)(2,1)S(1)}, u32[]{:S(2)}, u32[]{:S(2)}) collective-permute-start(bf16[2,128,256]{1,2,0:T(8,128)(2,1)S(1)} %pad_maximum_fusion.1), channel_id=1, source_target_pairs={{1,0},{2,1},{3,2},{4,3},{5,4},{6,5},{7,6},{8,7},{9,8},{10,9},{11,1... | collective-permute-start | bytes 393224 | tf_op jit(solution)/shard_map/ppermute | solution.py:12
  221.6 19.4 %all-to-all-start.4 = ((bf16[2,6,128,128]{3,0,1,2:T(2,128)(2,1)}), bf16[2,6,128,128]{3,0,1,2:T(2,128)(2,1)S(1)}, u32[]{:S(2)}, u32[]{:S(2)}) async-start(bf16[2,6,128,128]{3,0,1,2:T(2,128)(2,1)} %copy.66), calls=%async_computation.4 | async-start | bytes 786432 | tf_op jit(solution)/shard_map/all_to_all | solution.py:218
where the time goes:
time: 287 us; the launch traced here: 284 us
  matrix products  74.4 us (26%)
  waiting for transfers between devices  66.9 us (23%)
  starting transfers between devices  48.9 us (17%)
  local copies, waits for them, and re-layouts  44.8 us (16%)
  blocking collectives  34.1 us (12%)
  other arithmetic  13.5 us (5%)
    all_to_all x1, blocking collectives, shards(): lax.all_to_all(cut_home, 'tile', split_axis=0, concat_axis=0, tiled=True)  34.1 us
    dot_general x8, matrix products, add_group(): jnp.einsum('tbyo,tqo->byq', group_windows, build_tables(group_angles), pr...  33.5 us
    all_to_all x1, waiting for transfers between devices, shards(): lax.all_to_all(send_home, 'tile', split_axis=0, concat_axis=0, tiled=True)  25.4 us
    dot_general x8, matrix products, project_group(): jnp.einsum('byq,tqo->tbyo', flattened, build_tables(group_angles), prefer...  24.6 us
    all_to_all x1, waiting for transfers between devices, shards(): lax.all_to_all(back_items, 'tilt', split_axis=2, concat_axis=0, tiled=True)  13.9 us
    all_to_all x1, waiting for transfers between devices, shards(): lax.all_to_all(slab_projections, 'tilt', split_axis=0, concat_axis=2, til...  13.3 us
    ppermute x2, starting transfers between devices, extended_2(): after = lax.ppermute(leading, axis, down)  11.7 us
    gather x1, local copies, waits for them, and re-layouts, one_slot(): lax.dynamic_slice(extended, (slot_entry[0], base_row + slot_entry[1], 0),...  9.25 us
  transfers between devices with their start and end apart: 10, of which 8 were waited for; matrix products, arithmetic and copies ran while one was open for 6% of the time, Pallas kernels for 0%

commit v1 on v0

v1 whole, which is shorter than its diff:
```python
import functools

import jax
import jax.numpy as jnp
from jax import lax
from jax.experimental import pallas as pl
from jax.experimental.pallas import tpu as pltpu
from jax.sharding import PartitionSpec as P

HR = 8
MESH = pl.DeviceIdType.MESH
BF16 = jnp.bfloat16
F32 = jnp.float32
MIB = 1 << 20


def signal(device):
    pl.semaphore_signal(
        pltpu.get_barrier_semaphore(), inc=1, device_id=device, device_id_type=MESH
    )


def remote(src, dst, send_sem, recv_sem, device):
    return pltpu.make_async_remote_copy(
        src_ref=src, dst_ref=dst, send_sem=send_sem, recv_sem=recv_sem,
        device_id=device, device_id_type=MESH,
    )


def offsets_c_minus_x(transposed):
    rows = lax.broadcasted_iota(jnp.int32, (128, 128), 0)
    cols = lax.broadcasted_iota(jnp.int32, (128, 128), 1)
    return ((rows - cols) if transposed else (cols - rows)).astype(F32).astype(BF16)


def shear_block(tap, near, far, tilt, layer, apart):
    low = jnp.full((128, 128), tap[tilt, layer], F32).astype(BF16)
    high = jnp.full((128, 128), tap[tilt, layer] + 1.0, F32).astype(BF16)
    first = jnp.full((128, 128), near[tilt, layer], F32).astype(BF16)
    second = jnp.full((128, 128), far[tilt, layer], F32).astype(BF16)
    zero = jnp.zeros((128, 128), BF16)
    return jnp.where(apart == low, first, jnp.where(apart == high, second, zero))


def shear_tile(tap, near, far, tilt, layer, apart, transposed):
    make = lambda t, z: shear_block(tap, near, far, tilt + t, layer + z, apart)
    if transposed:
        parts = [[make(t, z) for z in range(2)] for t in range(2)]
    else:
        parts = [[make(t, z) for t in range(2)] for z in range(2)]
    return jnp.concatenate([jnp.concatenate(row, axis=1) for row in parts], axis=0)


def project_kernel(groups, tap, near, far, v_ref, out_ref, wide, pairs, sent, send_sems, recv_sems):
    me, tile = lax.axis_index("tilt"), lax.axis_index("tile")
    for d in range(1, groups):
        signal(((me + d) % groups, tile))
    rows = v_ref.shape[0]
    lines = rows // 64

    def widen(i, carry):
        at = pl.ds(pl.multiple_of(i * 512, 512), 512)
        wide[at, :] = v_ref[at, :].astype(F32)
        return carry

    lax.fori_loop(0, rows // 512, widen, 0)

    def gather(k, carry):
        even = wide[pl.ds(2 * k, lines, stride=64), :]
        odd = wide[pl.ds(2 * k + 1, lines, stride=64), :]
        pairs[k] = jnp.concatenate([even, odd], axis=1).astype(BF16)
        return carry

    lax.fori_loop(0, 32, gather, 0)
    pl.semaphore_wait(pltpu.get_barrier_semaphore(), groups - 1)
    apart = offsets_c_minus_x(False)
    copies = []
    for step in range(groups):
        d = 4 + step // 2 if step % 2 == 0 else 4 - (step + 1) // 2
        target = (me + d) % groups

        def add(k, acc):
            tile_w = shear_tile(tap, near, far, 2 * target, 2 * k, apart, False)
            return acc + jnp.dot(pairs[k], tile_w, preferred_element_type=F32)

        acc = lax.fori_loop(0, 32, add, jnp.zeros((lines, 256), F32), unroll=2)
        both = [acc[:, 128 * t : 128 * t + 128].astype(BF16).reshape(lines // 16, 16, 128) for t in range(2)]
        mine = pl.ds(pl.multiple_of(16 * me, 16), 16)
        if d == 0:
            for t in range(2):
                out_ref[t, :, mine, :] = both[t]
        else:
            for t in range(2):
                sent[step, t] = both[t]
            copy = remote(
                sent.at[step], out_ref.at[:, :, mine, :], send_sems.at[step], recv_sems.at[step], (target, tile)
            )
            copy.start()
            copies.append(copy)
    for copy in copies:
        copy.wait()


def place_kernel(rows_ref, cols_ref, w_ref, out_ref, canvas):
    tilts, boxes = w_ref.shape[:2]
    strips = out_ref.shape[1]

    def clear(i, carry):
        at = pl.ds(pl.multiple_of(i * 136, 8), 136)
        for t in range(tilts):
            canvas[t, at, :] = jnp.zeros((136, 256), F32)
        return carry

    lax.fori_loop(0, canvas.shape[1] // 136, clear, 0)
    for b in range(boxes):
        for t in range(tilts):
            row, col = rows_ref[b, t], cols_ref[b, t]
            window = jnp.concatenate([w_ref[t, b].astype(F32), jnp.zeros((128, 128), F32)], axis=1)
            window = pltpu.roll(window, col, 1)
            window = jnp.concatenate([window, jnp.zeros((8, 256), F32)], axis=0)
            window = pltpu.roll(window, row % 8, 0)
            at = pl.ds(pl.multiple_of(row // 8 * 8, 8), 136)
            canvas[t, at, :] = canvas[t, at, :] + window

    def narrow(i, carry):
        at = pl.ds(pl.multiple_of(i * 128, 128), 128)
        for t in range(tilts):
            out_ref[t, i] = canvas[t, at, :].astype(BF16)
        return carry

    lax.fori_loop(0, strips, narrow, 0)


def image_kernel(
    spread, can, measured, residual, img,
    r_a, s_b, o_b, f_b, s_c, o_c, f_c, own, table, pred_half, pred, halo, m_halo, res,
    a_sems, b_sems, c_sems, h_sems, g_sems,
):
    z, tile = lax.axis_index("tilt"), lax.axis_index("tile")
    x, y, c = tile // 8, (tile // 2) % 4, tile % 2
    other = 1 - c

    def dev(dx, dy):
        return (z, ((x + dx) % 4) * 8 + ((y + dy) % 4) * 2 + c)

    sibling = (z, x * 8 + y * 2 + other)
    below, above = (z, (tile + 1) % 32), (z, (tile + 31) % 32)
    right = lambda axis: dev(1, 0) if axis == 0 else dev(0, 1)
    left = lambda axis: dev(3, 0) if axis == 0 else dev(0, 3)
    place = (x, y)
    for device in (sibling, below, above, right(0), left(0), right(1), left(1)):
        signal(device)
    pl.semaphore_wait(pltpu.get_barrier_semaphore(), 7)

    steps = (2, 1, 3, 0)

    def block(ref, t, p, core):
        return ref.at[0, p, :, core] if t == 0 else ref.at[1, :, p, core]

    a_copies = {}
    for k, d in enumerate(steps):
        for t in range(2):
            p = (place[t] + d) % 4
            copy = remote(
                block(can, t, p, other), r_a.at[t, k], a_sems.at[0, t, k], a_sems.at[1, t, k], sibling
            )
            copy.start()
            a_copies[t, k] = copy
    m_copies = []
    for k, (device, start) in enumerate(((below, 120), (above, 0))):
        copy = remote(
            measured.at[:, pl.ds(start, 8), :], m_halo.at[k], h_sems.at[0, k], h_sems.at[1, k], device
        )
        copy.start()
        m_copies.append(copy)

    def fill(i, carry):
        lanes = lax.broadcasted_iota(jnp.int32, (16, 256), 1)
        subs = lax.broadcasted_iota(jnp.int32, (16, 256), 0) + i * 16
        apart = jnp.abs(lanes - subs).astype(F32).astype(BF16)
        masks = [apart == jnp.full((16, 256), j, F32).astype(BF16) for j in range(HR + 1)]
        for t in range(2):
            for a in range(HR + 1):
                value = jnp.zeros((16, 256), BF16)
                for j in range(HR + 1):
                    value = jnp.where(masks[j], jnp.full((16, 256), spread[t, a * (HR + 1) + j], F32).astype(BF16), value)
                table[t, a, pl.ds(pl.multiple_of(i * 16, 16), 16), :] = value
        return carry

    lax.fori_loop(0, 16, fill, 0)

    pending = []

    def go(src, dst, sems, t, k, device):
        copy = remote(src, dst, sems.at[0, t, k], sems.at[1, t, k], device)
        copy.start()
        pending.append(copy)
        return copy

    def local_b(t, k, half):
        d = steps[k]
        p = (place[t] + d) % 4
        at = pl.ds(2 * half, 2)
        mine = can[0, p, at, c] if t == 0 else can[1, at, p, c]
        return mine.astype(F32) + r_a[t, k, at].astype(F32)

    b_in = {}
    for t in range(2):
        a_copies[t, 0].wait_recv()
        for h, device in ((0, right(t)), (1, left(t))):
            s_b[t, 0, pl.ds(2 * h, 2)] = local_b(t, 0, h).astype(BF16)
            b_in[t, "opp", h] = go(s_b.at[t, 0, pl.ds(2 * h, 2)], o_b.at[t, h], b_sems, t, h, device)
    for t in range(2):
        for k, h, device in ((1, 1, right(t)), (2, 0, left(t))):
            a_copies[t, k].wait_recv()
            at = pl.ds(2 * h, 2)
            s_b[t, k, at] = local_b(t, k, h).astype(BF16)
            b_in[t, "free", k] = go(s_b.at[t, k, at], f_b.at[t, k - 1, at], b_sems, t, 1 + k, device)
    for t in range(2):
        for k, h, device in ((1, 0, right(t)), (2, 1, left(t))):
            at = pl.ds(2 * h, 2)
            b_in[t, "opp", h].wait_recv()
            s_b[t, k, at] = (local_b(t, k, h) + o_b[t, h].astype(F32)).astype(BF16)
            b_in[t, "bound", k] = go(s_b.at[t, k, at], f_b.at[t, k - 1, at], b_sems, t, 3 + k, device)
    for t in range(2):
        a_copies[t, 3].wait_recv()
        for h in range(2):
            own[t, pl.ds(2 * h, 2)] = local_b(t, 3, h)
        for k in (1, 2):
            b_in[t, "free", k].wait_recv()
            b_in[t, "bound", k].wait_recv()

    def local_c(t, k, half):
        q = (place[1 - t] + steps[k]) % 4
        at = pl.ds(64 * half, 64)
        return own[t, q, at, :] + f_b[t, 0, q, at, :].astype(F32) + f_b[t, 1, q, at, :].astype(F32)

    c_in = {}
    for t in range(2):
        for h, device in ((0, right(1 - t)), (1, left(1 - t))):
            at = pl.ds(64 * h, 64)
            s_c[t, 0, at] = local_c(t, 0, h).astype(BF16)
            c_in[t, "opp", h] = go(s_c.at[t, 0, at], o_c.at[t, h], c_sems, t, h, device)
        for k, h, device in ((1, 1, right(1 - t)), (2, 0, left(1 - t))):
            at = pl.ds(64 * h, 64)
            s_c[t, k, at] = local_c(t, k, h).astype(BF16)
            c_in[t, "free", k] = go(s_c.at[t, k, at], f_c.at[t, k - 1, at], c_sems, t, 1 + k, device)
    for t in range(2):
        for k, h, device in ((1, 0, right(1 - t)), (2, 1, left(1 - t))):
            at = pl.ds(64 * h, 64)
            c_in[t, "opp", h].wait_recv()
            s_c[t, k, at] = (local_c(t, k, h) + o_c[t, h].astype(F32)).astype(BF16)
            c_in[t, "bound", k] = go(s_c.at[t, k, at], f_c.at[t, k - 1, at], c_sems, t, 3 + k, device)
    for t in range(2):
        for k in (1, 2):
            c_in[t, "free", k].wait_recv()
            c_in[t, "bound", k].wait_recv()
        total = jnp.concatenate([local_c(t, 3, h) for h in range(2)], axis=0)
        total = total + f_c[t, 0].astype(F32) + f_c[t, 1].astype(F32)
        pred_half[t] = total.astype(BF16)
        pred[t, pl.ds(16, 128), :] = pred_half[t].astype(F32)

    p_copies = []
    for k, (device, start) in enumerate(((below, 112), (above, 0))):
        copy = remote(
            pred_half.at[:, pl.ds(start, 16), :], halo.at[k], h_sems.at[0, 2 + k], h_sems.at[1, 2 + k], device
        )
        copy.start()
        p_copies.append(copy)
    has_above = jnp.where(tile > 0, 1.0, 0.0).astype(F32)
    has_below = jnp.where(tile < 31, 1.0, 0.0).astype(F32)
    for copy in m_copies + p_copies:
        copy.wait_recv()
    for t in range(2):
        pred[t, pl.ds(0, 16), :] = halo[0, t].astype(F32) * has_above
        pred[t, pl.ds(144, 16), :] = halo[1, t].astype(F32) * has_below

    g_in = {}

    def give(t, bx, by, core, rows, k, device):
        at = pl.ds(rows[0], rows[1])
        where = img.at[t, bx, by, core, at]
        copy = remote(where, where, g_sems.at[0, t, k], g_sems.at[1, t, k], device)
        copy.start()
        pending.append(copy)
        return copy

    def at_place(t, p, q):
        return (p, q) if t == 0 else (q, p)

    for t in range(2):
        total = jnp.zeros((144, 256), F32)
        for i in range(2 * HR + 1):
            lhs = pred[t, pl.ds(i, 144), :].astype(BF16)
            total = total + jnp.dot(lhs, table[t, abs(i - HR)], preferred_element_type=F32)
        inner = measured[t] - total[8:136]
        residual[t] = inner
        res[t, pl.ds(8, 128), :] = inner.astype(BF16).astype(F32)
        res[t, pl.ds(0, 8), :] = (m_halo[0, t] - total[0:8]).astype(BF16).astype(F32) * has_above
        res[t, pl.ds(136, 8), :] = (m_halo[1, t] - total[136:144]).astype(BF16).astype(F32) * has_below
        total = jnp.zeros((128, 256), F32)
        for i in range(2 * HR + 1):
            lhs = res[t, pl.ds(i, 128), :].astype(BF16)
            total = total + jnp.dot(lhs, table[t, abs(i - HR)], preferred_element_type=F32)
        img[t, x, y, c] = total.astype(BF16)
        whole = (0, 128)
        g_in[t, "q", 0] = give(t, x, y, c, whole, 0, right(1 - t))
        g_in[t, "q", 1] = give(t, x, y, c, whole, 1, left(1 - t))
        g_in[t, "p", 0, 0] = give(t, x, y, c, whole, 4, right(t))
        g_in[t, "p", 0, 1] = give(t, x, y, c, whole, 5, left(t))
        g_in[t, "s", 0, 0] = give(t, x, y, c, whole, 20, sibling)

    def spread_block(t, dq, slot):
        q = (place[1 - t] + dq) % 4
        bx, by = at_place(t, place[t], q)
        g_in[t, "p", slot, 0] = give(t, bx, by, c, (0, 128), 4 + 4 * slot, right(t))
        g_in[t, "p", slot, 1] = give(t, bx, by, c, (0, 128), 5 + 4 * slot, left(t))
        g_in[t, "s", 0, slot] = give(t, bx, by, c, (0, 128), 20 + slot, sibling)

    for t in range(2):
        g_in[t, "q", 0].wait_recv()
        bx, by = at_place(t, place[t], (place[1 - t] + 3) % 4)
        g_in[t, "q", 2] = give(t, bx, by, c, (0, 64), 2, right(1 - t))
        g_in[t, "q", 1].wait_recv()
        bx2, by2 = at_place(t, place[t], (place[1 - t] + 1) % 4)
        g_in[t, "q", 3] = give(t, bx2, by2, c, (64, 64), 3, left(1 - t))
        spread_block(t, 3, 1)
        spread_block(t, 1, 2)
    for t in range(2):
        g_in[t, "q", 2].wait_recv()
        g_in[t, "q", 3].wait_recv()
        spread_block(t, 2, 3)

    offsets = (0, 3, 1, 2)
    for slot in range(4):
        for t in range(2):
            q = (place[1 - t] + offsets[slot]) % 4
            for side, (dp, start, device) in enumerate(((3, 0, right(t)), (1, 64, left(t)))):
                g_in[t, "p", slot, side].wait_recv()
                bx, by = at_place(t, (place[t] + dp) % 4, q)
                g_in[t, "f", slot, side] = give(t, bx, by, c, (start, 64), 6 + 4 * slot + side, device)
                g_in[t, "s", 1 + side, slot] = give(t, bx, by, c, (0, 128), 24 + 4 * side + slot, sibling)
    for slot in range(4):
        for t in range(2):
            q = (place[1 - t] + offsets[slot]) % 4
            g_in[t, "f", slot, 0].wait_recv()
            g_in[t, "f", slot, 1].wait_recv()
            bx, by = at_place(t, (place[t] + 2) % 4, q)
            g_in[t, "s", 3, slot] = give(t, bx, by, c, (0, 128), 32 + slot, sibling)
    for slot in range(4):
        for t in range(2):
            for column in range(4):
                g_in[t, "s", column, slot].wait_recv()
    for copy in list(a_copies.values()) + m_copies + p_copies + pending:
        copy.wait_send()


def cut_kernel(rows_ref, cols_ref, img, out_ref, wide):
    tilts, boxes = out_ref.shape[:2]
    last = img.shape[1] // 16 - 9
    for t in range(tilts):
        for b in range(boxes):
            wide[t * boxes + b, pl.ds(144, 128), :] = jnp.zeros((128, 256), F32)
    for t in range(tilts):
        for b in range(boxes):
            slot = t * boxes + b
            row, col = rows_ref[b, t], cols_ref[b, t]
            top = jnp.minimum(row // 16, last) * 16
            wide[slot, pl.ds(0, 144), :] = img[t, pl.ds(pl.multiple_of(top, 16), 144), :].astype(F32)
            off = row - top
            rough = wide[slot, pl.ds(pl.multiple_of(off // 8 * 8, 8), 136), :]
            fine = pltpu.roll(rough, 136 - off % 8, 0)[:128]
            out_ref[t, b] = pltpu.roll(fine, 256 - col, 1)[:, :128].astype(BF16)


def exchange_kernel(groups, windows, out_ref, send_sems, recv_sems):
    me, tile = lax.axis_index("tilt"), lax.axis_index("tile")
    for d in range(1, groups):
        signal(((me + d) % groups, tile))
    pl.semaphore_wait(pltpu.get_barrier_semaphore(), groups - 1)
    copies = []
    for k, d in enumerate((4, 3, 5, 2, 6, 1, 7)):
        target = (me + d) % groups
        copy = remote(
            windows.at[:, :, pl.ds(pl.multiple_of(16 * target, 16), 16), :], out_ref.at[me],
            send_sems.at[k], recv_sems.at[k], (target, tile),
        )
        copy.start()
        copies.append(copy)
    out_ref[me] = windows[:, :, pl.ds(pl.multiple_of(16 * me, 16), 16), :]
    for copy in copies:
        copy.wait()


def back_kernel(scale, tap, near, far, rows_ref, out_ref, lines):
    step = pl.program_id(0)

    @pl.when(step == 0)
    def _():
        for t in range(rows_ref.shape[0]):
            lines[t // 2, :, pl.ds(128 * (t % 2), 128)] = rows_ref[t]

    apart = offsets_c_minus_x(True)
    depth = out_ref.shape[1]
    for k in range(depth // 2):
        layer = step * depth + 2 * k

        def add(g, acc):
            tile_w = shear_tile(tap, near, far, 2 * g, layer, apart, True)
            return acc + jnp.dot(lines[g], tile_w, preferred_element_type=F32)

        acc = lax.fori_loop(0, lines.shape[0], add, jnp.zeros((lines.shape[1], 256), F32), unroll=2)
        acc = acc * scale
        out_ref[:, 2 * k, :] = acc[:, :128]
        out_ref[:, 2 * k + 1, :] = acc[:, 128:]


VMEM = pl.BlockSpec(memory_space=pltpu.VMEM)
SMEM = pl.BlockSpec(memory_space=pltpu.SMEM)


def call_project(volumes, tables, groups):
    boxes, slab, depth, width = volumes.shape
    lines = boxes * slab
    return pl.pallas_call(
        functools.partial(project_kernel, groups),
        out_shape=jax.ShapeDtypeStruct((2, boxes, slab * groups, width), BF16),
        in_specs=[SMEM] * 3 + [VMEM],
        out_specs=VMEM,
        scratch_shapes=[
            pltpu.VMEM((lines * depth, width), F32),
            pltpu.VMEM((depth // 2, lines, 2 * width), BF16),
            pltpu.VMEM((groups, 2, boxes, slab, width), BF16),
            pltpu.SemaphoreType.DMA((groups,)),
            pltpu.SemaphoreType.DMA((groups,)),
        ],
        compiler_params=pltpu.CompilerParams(
            collective_id=0, has_side_effects=True, vmem_limit_bytes=32 * MIB
        ),
    )(*tables, volumes.reshape(lines * depth, width))


def call_place(windows, rows, cols, strips):
    return pl.pallas_call(
        place_kernel,
        out_shape=jax.ShapeDtypeStruct((2, strips, 128, 256), BF16),
        in_specs=[SMEM, SMEM, VMEM],
        out_specs=VMEM,
        scratch_shapes=[pltpu.VMEM((2, (strips + 1) * 128 + 128, 256), F32)],
        compiler_params=pltpu.CompilerParams(vmem_limit_bytes=40 * MIB),
    )(rows, cols, windows)


def call_image(canvas, spread, measured):
    dma = lambda *shape: pltpu.SemaphoreType.DMA(shape)
    blocks = lambda *shape: pltpu.VMEM(shape, BF16)
    return pl.pallas_call(
        image_kernel,
        out_shape=(
            jax.ShapeDtypeStruct((2, 128, 256), F32),
            jax.ShapeDtypeStruct((2, 4, 4, 2, 128, 256), BF16),
        ),
        in_specs=[SMEM, VMEM, VMEM],
        out_specs=(VMEM, VMEM),
        scratch_shapes=[
            blocks(2, 4, 4, 128, 256),
            blocks(2, 3, 4, 128, 256),
            blocks(2, 2, 2, 128, 256),
            blocks(2, 2, 4, 128, 256),
            blocks(2, 3, 128, 256),
            blocks(2, 2, 64, 256),
            blocks(2, 2, 128, 256),
            pltpu.VMEM((2, 4, 128, 256), F32),
            blocks(2, 9, 256, 256),
            blocks(2, 128, 256),
            pltpu.VMEM((2, 160, 256), F32),
            blocks(2, 2, 16, 256),
            pltpu.VMEM((2, 2, 8, 256), F32),
            pltpu.VMEM((2, 144, 256), F32),
            dma(2, 2, 4),
            dma(2, 2, 6),
            dma(2, 2, 6),
            dma(2, 4),
            dma(2, 2, 36),
        ],
        compiler_params=pltpu.CompilerParams(
            collective_id=1, has_side_effects=True, vmem_limit_bytes=48 * MIB
        ),
    )(spread, canvas.reshape(2, 4, 4, 2, 128, 256), measured)


def call_cut(image, rows, cols):
    boxes, tilts = rows.shape
    return pl.pallas_call(
        cut_kernel,
        out_shape=jax.ShapeDtypeStruct((tilts, boxes, 128, 128), BF16),
        in_specs=[SMEM, SMEM, VMEM],
        out_specs=VMEM,
        scratch_shapes=[pltpu.VMEM((tilts * boxes, 272, 256), F32)],
        compiler_params=pltpu.CompilerParams(vmem_limit_bytes=32 * MIB),
    )(rows, cols, image.reshape(2, 4096, 256))


def call_exchange(windows, groups):
    tilts, boxes = windows.shape[:2]
    return pl.pallas_call(
        functools.partial(exchange_kernel, groups),
        out_shape=jax.ShapeDtypeStruct((groups, tilts, boxes, 16, 128), BF16),
        in_specs=[VMEM],
        out_specs=VMEM,
        scratch_shapes=[pltpu.SemaphoreType.DMA((7,)), pltpu.SemaphoreType.DMA((7,))],
        compiler_params=pltpu.CompilerParams(
            collective_id=2, has_side_effects=True, vmem_limit_bytes=32 * MIB
        ),
    )(windows)


def call_back(back_rows, tables, shape):
    boxes, slab, depth, width = shape
    lines = boxes * slab
    tilts = back_rows.shape[0] * 2
    per_step = 8
    return pl.pallas_call(
        functools.partial(back_kernel, 1.0 / tilts),
        grid=(depth // per_step,),
        out_shape=jax.ShapeDtypeStruct((lines, depth, width), F32),
        in_specs=[SMEM] * 3 + [pl.BlockSpec((tilts, lines, width), lambda i: (0, 0, 0))],
        out_specs=pl.BlockSpec((lines, per_step, width), lambda i: (0, i, 0)),
        scratch_shapes=[pltpu.VMEM((tilts // 2, lines, 2 * width), BF16)],
        compiler_params=pltpu.CompilerParams(vmem_limit_bytes=32 * MIB),
    )(*tables, back_rows.reshape(tilts, lines, width)).reshape(shape)


def shear_tables(angles, depth):
    layers = jnp.arange(depth, dtype=F32)
    shift = (layers - (depth - 1) / 2.0) * jnp.sin(angles)[:, None]
    tap = jnp.floor(shift)
    weight = lambda offset: jnp.maximum(0.0, 1.0 - jnp.abs(offset - shift)).astype(BF16).astype(F32)
    return tap, weight(tap), weight(tap + 1.0)


def spread_table(defocus):
    steps = jnp.arange(HR + 1, dtype=F32)
    rho_sq = (steps[:, None] ** 2 + steps[None, :] ** 2).reshape(1, -1)
    scale = float(HR * HR)
    values = jnp.exp(-rho_sq / (2.0 * scale)) * jnp.cos(defocus[:, None] * rho_sq) / scale
    return values.astype(BF16).astype(F32)


def shards(volumes, angles, defocus, row_offsets, col_offsets, measured):
    groups = lax.axis_size("tilt")
    tables = shear_tables(angles, volumes.shape[2])
    windows = call_project(volumes, tables, groups)
    canvas = call_place(windows, row_offsets, col_offsets, lax.axis_size("tile"))
    residual, image = call_image(canvas, spread_table(defocus), measured)
    back_rows = call_exchange(call_cut(image, row_offsets, col_offsets), groups)
    return residual, call_back(back_rows, tables, volumes.shape)


def solution(mesh):
    in_specs = (
        P("tile", "tilt", None, None),
        P(),
        P("tilt"),
        P("tile", "tilt"),
        P("tile", "tilt"),
        P("tilt", "tile", None),
    )
    out_specs = (P("tilt", "tile", None), P("tile", "tilt", None, None))
    return jax.shard_map(shards, mesh=mesh, in_specs=in_specs, out_specs=out_specs, check_vma=False)
```

time: 287 us -> 138 us (0.48)
  Pallas kernels: 0 us -> 130 us
  matrix products: 74.4 us -> 0 us
  waiting for transfers between devices: 66.9 us -> 0 us
  starting transfers between devices: 48.9 us -> 0 us
  local copies, waits for them, and re-layouts: 44.8 us -> 6.36 us
  blocking collectives: 34.1 us -> 0 us
  other arithmetic: 13.5 us -> 0.95 us
    pallas_call x0 -> x6, Pallas kernels: none -> 130 us  [the longest x1 48.7 us: call_image(): pl.pallas_call(image_kernel, out_shape=(jax.ShapeDtypeStruct((2, 128, 256...]
    dot_general x25 -> x0, matrix products: 74.4 us -> none  [the longest x8 33.5 us: add_group(): jnp.einsum('tbyo,tqo->byq', group_windows, build_tables(group_angles), pr...]
    all_to_all x4 -> x0, waiting for transfers between devices: 55.8 us -> none  [the longest x1 25.4 us: shards(): lax.all_to_all(send_home, 'tile', split_axis=0, concat_axis=0, tiled=True)]
    all_to_all x1 -> x0, blocking collectives: 34.1 us -> none  [shards(): lax.all_to_all(cut_home, 'tile', split_axis=0, concat_axis=0, tiled=True)]
    all_to_all x4 -> x0, starting transfers between devices: 24.9 us -> none  [the longest x1 8.47 us: shards(): lax.all_to_all(slab_projections, 'tilt', split_axis=0, concat_axis=2, til...]
    ppermute x6 -> x0, starting transfers between devices: 24 us -> none  [the longest x2 11.7 us: extended_2(): after = lax.ppermute(leading, axis, down)]
    ppermute x6 -> x0, waiting for transfers between devices: 11.1 us -> none  [the longest x2 8.64 us: from_behind(): return lax.ppermute(block, axis, route)]
    convert_element_type x5 -> x2, other arithmetic: 10.1 us -> 0.85 us  [the longest x1 0.77 us: spread_table(): return values.astype(BF16).astype(F32)]
  transfers between devices with their start and end apart: 10 -> 0, of which waited for: 8 -> 0; matrix products, arithmetic and copies ran while one was open for 6% -> 0% of each run, Pallas kernels for 0% -> 0%
where the time goes in v1:
time: 138 us
  Pallas kernels  130 us (94%)
  local copies, waits for them, and re-layouts  6.36 us (5%)
    pallas_call x1, Pallas kernels, call_image(): pl.pallas_call(image_kernel, out_shape=(jax.ShapeDtypeStruct((2, 128, 256...  48.7 us
    pallas_call x1, Pallas kernels, call_project(): pl.pallas_call(functools.partial(project_kernel, groups), out_shape=jax.S...  33.7 us
    pallas_call x1, Pallas kernels, call_back(): pl.pallas_call(functools.partial(back_kernel, 1.0 / tilts), grid=(depth /...  29.1 us
    pallas_call x1, Pallas kernels, call_exchange(): pl.pallas_call(functools.partial(exchange_kernel, groups), out_shape=jax....  14.1 us
    unnamed x9, local copies, waits for them, and re-layouts  5.58 us

profile of v1, /device:TPU:2, one launch (start us, length us, event | category | flops | bytes accessed | tf_op | source)
XLA Modules:
  0.0 137.7 jit_solution(5644985468038890167)
XLA Ops:
  0.6 0.7 sin.3
  1.3 0.8 copy.8.rows_ref
  2.1 0.8 copy.9.cols_ref
  2.9 0.1 broadcast_add_fusion
  3.0 0.1 add.43
  3.0 0.8 fusion.10.spread
  3.8 0.1 fusion.8
  3.9 0.0 copy-start.1
  3.9 1.4 %copy-done.1 = bf16[6,16,64,128]{3,2,1,0:T(8,128)(2,1)S(1)} copy-done((bf16[6,16,64,128]{3,2,1,0:T(8,128)(2,1)S(1)}, bf16[6,16,64,128]{3,2,1,0:T(8,128)(2,1)}, u32[]{:S(2)}) %copy-start.1) | copy-done | bytes 1572888
  5.3 0.0 copy-start.2
  5.3 33.7 %shard_map.77.w_ref = bf16[2,6,128,128]{3,2,1,0:T(8,128)(2,1)S(1)} custom-call(f32[16,64]{1,0:T(8,128)S(1)} %get-tuple-element.8.tap, f32[16,64]{1,0:T(8,128)S(1)} %get-tuple-element.7.near, f32[16,64]{1,0:T(8,128)S(1)} %get-tuple-element.6.far, bf16[6144,128]{1,0:T(8,128)(2,1)S(1)} %bitcast.8), custom_call_target="tpu_custom_call" | custom-call | tf_op jit(solution)/shard_map/pallas_call | solution.py:425
  39.0 2.6 %shard_map.78 = bf16[2,32,128,256]{3,2,1,0:T(8,128)(2,1)S(1)} custom-call(s32[6,2]{1,0:T(8,128)S(1)} %copy.8.rows_ref, s32[6,2]{1,0:T(8,128)S(1)} %copy.9.cols_ref, bf16[2,6,128,128]{3,2,1,0:T(8,128)(2,1)S(1)} %shard_map.77.w_ref), custom_call_target="tpu_custom_call" | custom-call | tf_op jit(solution)/shard_map/pallas_call | solution.py:444
  41.6 0.0 copy-start
  41.6 1.9 %copy-done = bf16[2,32,128,256]{3,2,1,0:T(8,128)(2,1)} copy-done((bf16[2,32,128,256]{3,2,1,0:T(8,128)(2,1)}, bf16[2,32,128,256]{3,2,1,0:T(8,128)(2,1)S(1)}, u32[]{:S(2)}) %copy-start) | copy-done | bytes 4194328
  43.5 0.0 copy-done.2
  43.6 48.7 %shard_map.79 = (f32[2,128,256]{2,1,0:T(8,128)S(1)}, bf16[2,4,4,2,128,256]{5,4,3,2,1,0:T(8,128)(2,1)S(1)}) custom-call(f32[2,81]{1,0:T(2,128)S(1)} %fusion.10.spread, bf16[2,4,4,2,128,256]{5,4,3,2,1,0:T(8,128)(2,1)} %bitcast.5, f32[2,128,256]{2,1,0:T(8,128)S(1)} %copy-done.2), custom_call_target="tpu_custom_call" | custom-call | tf_op jit(solution)/shard_map/pallas_call | solution.py:457
  92.3 1.5 %shard_map.80.windows = bf16[2,6,128,128]{3,2,1,0:T(8,128)(2,1)S(1)} custom-call(s32[6,2]{1,0:T(8,128)S(1)} %copy.8.rows_ref, s32[6,2]{1,0:T(8,128)S(1)} %copy.9.cols_ref, bf16[2,4096,256]{2,1,0:T(8,128)(2,1)S(1)} %bitcast.6), custom_call_target="tpu_custom_call" | custom-call | tf_op jit(solution)/shard_map/pallas_call | solution.py:494
  93.8 14.1 %shard_map.81 = bf16[8,2,6,16,128]{4,3,2,1,0:T(8,128)(2,1)S(1)} custom-call(bf16[2,6,128,128]{3,2,1,0:T(8,128)(2,1)S(1)} %shard_map.80.windows), custom_call_target="tpu_custom_call" | custom-call | tf_op jit(solution)/shard_map/pallas_call | solution.py:506
  107.9 29.1 %shard_map.82 = f32[96,64,128]{2,1,0:T(8,128)} custom-call(f32[16,64]{1,0:T(8,128)S(1)} %get-tuple-element.8.tap, f32[16,64]{1,0:T(8,128)S(1)} %get-tuple-element.7.near, f32[16,64]{1,0:T(8,128)S(1)} %get-tuple-element.6.far, bf16[16,96,128]{2,1,0:T(8,128)(2,1)S(1)} %bitcast.7), custom_call_target="tpu_custom_call" | custom-call | tf_op jit(solution)/shard_map/pallas_call | solution.py:523
  137.0 0.7 copy.13
  (3 shorter events, 0.0 us)
Async XLA Ops:
  3.9 1.4 %copy-start.1 = (bf16[6,16,64,128]{3,2,1,0:T(8,128)(2,1)S(1)}, bf16[6,16,64,128]{3,2,1,0:T(8,128)(2,1)}, u32[]{:S(2)}) copy-start(bf16[6,16,64,128]{3,2,1,0:T(8,128)(2,1)} %param.6) | copy-start | bytes 4718596
  5.3 38.2 %copy-start.2 = (f32[2,128,256]{2,1,0:T(8,128)S(1)}, f32[2,128,256]{2,1,0:T(8,128)}, u32[]{:S(2)}) copy-start(f32[2,128,256]{2,1,0:T(8,128)} %measured.1) | copy-start | bytes 786436
  41.6 1.9 %copy-start = (bf16[2,32,128,256]{3,2,1,0:T(8,128)(2,1)}, bf16[2,32,128,256]{3,2,1,0:T(8,128)(2,1)S(1)}, u32[]{:S(2)}) copy-start(bf16[2,32,128,256]{3,2,1,0:T(8,128)(2,1)S(1)} %shard_map.78) | copy-start | bytes 12582916

commit v2 on v1

--- a/solution.py
+++ b/solution.py
@@ -33,17 +33,32 @@
     return ((rows - cols) if transposed else (cols - rows)).astype(F32).astype(BF16)
 
 
-def shear_block(tap, near, far, tilt, layer, apart):
-    low = jnp.full((128, 128), tap[tilt, layer], F32).astype(BF16)
-    high = jnp.full((128, 128), tap[tilt, layer] + 1.0, F32).astype(BF16)
-    first = jnp.full((128, 128), near[tilt, layer], F32).astype(BF16)
-    second = jnp.full((128, 128), far[tilt, layer], F32).astype(BF16)
+def sine(x):
+    square = x * x
+    value = -1.0 / 39916800.0 + square * (1.0 / 6227020800.0)
+    for factor in (1.0 / 362880.0, -1.0 / 5040.0, 1.0 / 120.0, -1.0 / 6.0):
+        value = factor + square * value
+    return x + x * (square * value)
+
+
+def sines_into(angles, sines):
+    for t in range(angles.shape[0]):
+        sines[t] = sine(angles[t])
+
+
+def shear_block(sines, tilt, layer, apart):
+    shift = (jnp.asarray(layer, jnp.int32).astype(F32) - 31.5) * sines[tilt]
+    tap = shift.astype(jnp.int32).astype(F32)
+    tap = jnp.where(tap > shift, tap - 1.0, tap)
+    all_of = lambda value: jnp.full((128, 128), value, F32).astype(BF16)
+    near = jnp.maximum(0.0, 1.0 - jnp.abs(tap - shift))
+    far = jnp.maximum(0.0, 1.0 - jnp.abs(tap + 1.0 - shift))
     zero = jnp.zeros((128, 128), BF16)
-    return jnp.where(apart == low, first, jnp.where(apart == high, second, zero))
-
-
-def shear_tile(tap, near, far, tilt, layer, apart, transposed):
-    make = lambda t, z: shear_block(tap, near, far, tilt + t, layer + z, apart)
+    return jnp.where(apart == all_of(tap), all_of(near), jnp.where(apart == all_of(tap + 1.0), all_of(far), zero))
+
+
+def shear_tile(sines, tilt, layer, apart, transposed):
+    make = lambda t, z: shear_block(sines, tilt + t, layer + z, apart)
     if transposed:
         parts = [[make(t, z) for z in range(2)] for t in range(2)]
     else:
@@ -51,10 +66,25 @@
     return jnp.concatenate([jnp.concatenate(row, axis=1) for row in parts], axis=0)
 
 
-def project_kernel(groups, tap, near, far, v_ref, out_ref, wide, pairs, sent, send_sems, recv_sems):
+def flip_matrix():
+    rows = lax.broadcasted_iota(jnp.int32, (128, 128), 0)
+    cols = lax.broadcasted_iota(jnp.int32, (128, 128), 1)
+    return jnp.where(rows + cols == 127, 1.0, 0.0).astype(BF16)
+
+
+def flipped(x, flip):
+    high = x.astype(BF16)
+    low = (x - high.astype(F32)).astype(BF16)
+    return jnp.dot(
+        jnp.concatenate([high, low], axis=1), jnp.concatenate([flip, flip], axis=0), preferred_element_type=F32
+    )
+
+
+def project_kernel(groups, angles, v_ref, out_ref, sines, wide, pairs, sent, send_sems, recv_sems):
     me, tile = lax.axis_index("tilt"), lax.axis_index("tile")
     for d in range(1, groups):
         signal(((me + d) % groups, tile))
+    sines_into(angles, sines)
     rows = v_ref.shape[0]
     lines = rows // 64
 
@@ -64,41 +94,56 @@
         return carry
 
     lax.fori_loop(0, rows // 512, widen, 0)
+    flip = flip_matrix()
 
     def gather(k, carry):
-        even = wide[pl.ds(2 * k, lines, stride=64), :]
-        odd = wide[pl.ds(2 * k + 1, lines, stride=64), :]
-        pairs[k] = jnp.concatenate([even, odd], axis=1).astype(BF16)
-        return carry
-
-    lax.fori_loop(0, 32, gather, 0)
+        layer = lambda z: wide[pl.ds(z, lines, stride=64), :]
+        top = jnp.concatenate([layer(2 * k), layer(2 * k + 1)], axis=1).astype(BF16)
+        mirror = jnp.concatenate([layer(63 - 2 * k), layer(62 - 2 * k)], axis=0).astype(BF16)
+        mirror = jnp.dot(mirror, flip, preferred_element_type=F32).astype(BF16)
+        pairs[k] = jnp.concatenate([top, jnp.concatenate([mirror[:lines], mirror[lines:]], axis=1)], axis=0)
+        return carry
+
+    lax.fori_loop(0, 16, gather, 0)
     pl.semaphore_wait(pltpu.get_barrier_semaphore(), groups - 1)
     apart = offsets_c_minus_x(False)
-    copies = []
-    for step in range(groups):
-        d = 4 + step // 2 if step % 2 == 0 else 4 - (step + 1) // 2
+    mine = pl.ds(pl.multiple_of(16 * me, 16), 16)
+
+    def windows_of(target):
+        acc = jnp.zeros((2 * lines, 256), F32)
+        for k in range(16):
+            acc = acc + jnp.dot(
+                pairs[k], shear_tile(sines, 2 * target, 2 * k, apart, False), preferred_element_type=F32
+            )
+        mirror = flipped(jnp.concatenate([acc[lines:, :128], acc[lines:, 128:]], axis=0), flip)
+        both = (acc[:lines, :128] + mirror[:lines], acc[:lines, 128:] + mirror[lines:])
+        return [half.astype(BF16).reshape(lines // 16, 16, 128) for half in both]
+
+    def copy_of(step):
+        d = jnp.where(step % 2 == 0, 4 + step // 2, 4 - (step + 1) // 2)
         target = (me + d) % groups
-
-        def add(k, acc):
-            tile_w = shear_tile(tap, near, far, 2 * target, 2 * k, apart, False)
-            return acc + jnp.dot(pairs[k], tile_w, preferred_element_type=F32)
-
-        acc = lax.fori_loop(0, 32, add, jnp.zeros((lines, 256), F32), unroll=2)
-        both = [acc[:, 128 * t : 128 * t + 128].astype(BF16).reshape(lines // 16, 16, 128) for t in range(2)]
-        mine = pl.ds(pl.multiple_of(16 * me, 16), 16)
-        if d == 0:
-            for t in range(2):
-                out_ref[t, :, mine, :] = both[t]
-        else:
-            for t in range(2):
-                sent[step, t] = both[t]
-            copy = remote(
-                sent.at[step], out_ref.at[:, :, mine, :], send_sems.at[step], recv_sems.at[step], (target, tile)
-            )
-            copy.start()
-            copies.append(copy)
-    for copy in copies:
-        copy.wait()
+        return target, remote(
+            sent.at[step], out_ref.at[:, :, mine, :], send_sems.at[step], recv_sems.at[step], (target, tile)
+        )
+
+    def project(step, carry):
+        target, copy = copy_of(step)
+        both = windows_of(target)
+        for t in range(2):
+            sent[step, t] = both[t]
+        copy.start()
+        return carry
+
+    lax.fori_loop(0, groups - 1, project, 0)
+    both = windows_of(me)
+    for t in range(2):
+        out_ref[t, :, mine, :] = both[t]
+
+    def finish(step, carry):
+        copy_of(step)[1].wait()
+        return carry
+
+    lax.fori_loop(0, groups - 1, finish, 0)
 
 
 def place_kernel(rows_ref, cols_ref, w_ref, out_ref, canvas):
@@ -114,7 +159,7 @@
     lax.fori_loop(0, canvas.shape[1] // 136, clear, 0)
     for b in range(boxes):
         for t in range(tilts):
-            row, col = rows_ref[b, t], cols_ref[b, t]
+            row, col = rows_ref[t, b], cols_ref[t, b]
             window = jnp.concatenate([w_ref[t, b].astype(F32), jnp.zeros((128, 128), F32)], axis=1)
             window = pltpu.roll(window, col, 1)
             window = jnp.concatenate([window, jnp.zeros((8, 256), F32)], axis=0)
@@ -132,7 +177,7 @@
 
 
 def image_kernel(
-    spread, can, measured, residual, img,
+    defocus, can, measured, residual, img, spread_wide, spread,
     r_a, s_b, o_b, f_b, s_c, o_c, f_c, own, table, pred_half, pred, halo, m_halo, res,
     a_sems, b_sems, c_sems, h_sems, g_sems,
 ):
@@ -174,6 +219,16 @@
         copy.start()
         m_copies.append(copy)
 
+    down = lax.broadcasted_iota(jnp.int32, (16, 128), 0).astype(F32)
+    along = lax.broadcasted_iota(jnp.int32, (16, 128), 1).astype(F32)
+    rho_sq = down * down + along * along
+    scale = float(HR * HR)
+    for t in range(2):
+        spread_wide[t] = jnp.exp(-rho_sq / (2.0 * scale)) * jnp.cos(defocus[t] * rho_sq) / scale
+    to_scalars = pltpu.make_async_copy(spread_wide, spread, h_sems.at[0, 4])
+    to_scalars.start()
+    to_scalars.wait()
+
     def fill(i, carry):
         lanes = lax.broadcasted_iota(jnp.int32, (16, 256), 1)
         subs = lax.broadcasted_iota(jnp.int32, (16, 256), 0) + i * 16
@@ -183,7 +238,7 @@
             for a in range(HR + 1):
                 value = jnp.zeros((16, 256), BF16)
                 for j in range(HR + 1):
-                    value = jnp.where(masks[j], jnp.full((16, 256), spread[t, a * (HR + 1) + j], F32).astype(BF16), value)
+                    value = jnp.where(masks[j], jnp.full((16, 256), spread[t, a, j], F32).astype(BF16), value)
                 table[t, a, pl.ds(pl.multiple_of(i * 16, 16), 16), :] = value
         return carry
 
@@ -364,7 +419,7 @@
     for t in range(tilts):
         for b in range(boxes):
             slot = t * boxes + b
-            row, col = rows_ref[b, t], cols_ref[b, t]
+            row, col = rows_ref[t, b], cols_ref[t, b]
             top = jnp.minimum(row // 16, last) * 16
             wide[slot, pl.ds(0, 144), :] = img[t, pl.ds(pl.multiple_of(top, 16), 144), :].astype(F32)
             off = row - top
@@ -373,71 +428,115 @@
             out_ref[t, b] = pltpu.roll(fine, 256 - col, 1)[:, :128].astype(BF16)
 
 
-def exchange_kernel(groups, windows, out_ref, send_sems, recv_sems):
+def back_kernel(groups, scale, angles, windows, out_ref, sines, got, lines, sums, blocks, send_sems, recv_sems, sems):
     me, tile = lax.axis_index("tilt"), lax.axis_index("tile")
     for d in range(1, groups):
         signal(((me + d) % groups, tile))
+    sines_into(angles, sines)
+    flip = flip_matrix()
+    count = lines.shape[1] // 2
     pl.semaphore_wait(pltpu.get_barrier_semaphore(), groups - 1)
-    copies = []
-    for k, d in enumerate((4, 3, 5, 2, 6, 1, 7)):
+    copies = {}
+    for d in (1, 7, 2, 6, 3, 5, 4):
         target = (me + d) % groups
-        copy = remote(
-            windows.at[:, :, pl.ds(pl.multiple_of(16 * target, 16), 16), :], out_ref.at[me],
-            send_sems.at[k], recv_sems.at[k], (target, tile),
+        copies[d] = remote(
+            windows.at[:, :, pl.ds(pl.multiple_of(16 * target, 16), 16), :], got.at[d],
+            send_sems.at[d], recv_sems.at[d], (target, tile),
         )
-        copy.start()
-        copies.append(copy)
-    out_ref[me] = windows[:, :, pl.ds(pl.multiple_of(16 * me, 16), 16), :]
-    for copy in copies:
-        copy.wait()
-
-
-def back_kernel(scale, tap, near, far, rows_ref, out_ref, lines):
-    step = pl.program_id(0)
-
-    @pl.when(step == 0)
-    def _():
-        for t in range(rows_ref.shape[0]):
-            lines[t // 2, :, pl.ds(128 * (t % 2), 128)] = rows_ref[t]
-
+        copies[d].start()
     apart = offsets_c_minus_x(True)
-    depth = out_ref.shape[1]
-    for k in range(depth // 2):
-        layer = step * depth + 2 * k
-
-        def add(g, acc):
-            tile_w = shear_tile(tap, near, far, 2 * g, layer, apart, True)
-            return acc + jnp.dot(lines[g], tile_w, preferred_element_type=F32)
-
-        acc = lax.fori_loop(0, lines.shape[0], add, jnp.zeros((lines.shape[1], 256), F32), unroll=2)
-        acc = acc * scale
-        out_ref[:, 2 * k, :] = acc[:, :128]
-        out_ref[:, 2 * k + 1, :] = acc[:, 128:]
+
+    def take(slot, rows):
+        for t in range(2):
+            at = pl.ds(128 * t, 128)
+            line = rows[t].reshape(count, 128)
+            lines[slot, pl.ds(0, count), at] = line
+            lines[slot, pl.ds(count, count), at] = jnp.dot(line, flip, preferred_element_type=F32).astype(BF16)
+
+    def copies_of(i):
+        low = pltpu.make_async_copy(
+            blocks.at[0, i], out_ref.at[:, pl.ds(pl.multiple_of(8 * i, 8), 8), :], sems.at[0, i]
+        )
+        high = pltpu.make_async_copy(
+            blocks.at[1, i], out_ref.at[:, pl.ds(pl.multiple_of(56 - 8 * i, 8), 8), :], sems.at[1, i]
+        )
+        return low, high
+
+    order = ((0, 1), (7, 2), (6, 3), (5, 4))
+    for stage, pair in enumerate(order):
+        for slot, d in enumerate(pair):
+            if d == 0:
+                take(slot, windows[:, :, pl.ds(pl.multiple_of(16 * me, 16), 16), :])
+            else:
+                copies[d].wait_recv()
+                take(slot, got[d])
+        from_group = [(me - d + groups) % groups for d in pair]
+
+        def product(i, k):
+            acc = jnp.zeros((2 * count, 256), F32)
+            for slot in range(2):
+                weights = shear_tile(sines, 2 * from_group[slot], 8 * i + 2 * k, apart, True)
+                acc = acc + jnp.dot(lines[slot], weights, preferred_element_type=F32)
+            return acc
+
+        def first(i, carry):
+            for k in range(4):
+                sums[4 * i + k] = product(i, k)
+            return carry
+
+        def middle(i, carry):
+            for k in range(4):
+                sums[4 * i + k] = sums[4 * i + k] + product(i, k)
+            return carry
+
+        def last(i, carry):
+            for k in range(4):
+                acc = (sums[4 * i + k] + product(i, k)) * scale
+                blocks[0, i, :, 2 * k, :] = acc[:count, :128]
+                blocks[0, i, :, 2 * k + 1, :] = acc[:count, 128:]
+                mirror = flipped(jnp.concatenate([acc[count:, :128], acc[count:, 128:]], axis=0), flip)
+                blocks[1, i, :, 7 - 2 * k, :] = mirror[:count]
+                blocks[1, i, :, 6 - 2 * k, :] = mirror[count:]
+            for copy in copies_of(i):
+                copy.start()
+            return carry
+
+        lax.fori_loop(0, 4, first if stage == 0 else last if stage == 3 else middle, 0)
+
+    def finish(i, carry):
+        for copy in copies_of(i):
+            copy.wait()
+        return carry
+
+    lax.fori_loop(0, 4, finish, 0)
+    for copy in copies.values():
+        copy.wait_send()
 
 
 VMEM = pl.BlockSpec(memory_space=pltpu.VMEM)
 SMEM = pl.BlockSpec(memory_space=pltpu.SMEM)
 
 
-def call_project(volumes, tables, groups):
+def call_project(volumes, angles, groups):
     boxes, slab, depth, width = volumes.shape
     lines = boxes * slab
     return pl.pallas_call(
         functools.partial(project_kernel, groups),
         out_shape=jax.ShapeDtypeStruct((2, boxes, slab * groups, width), BF16),
-        in_specs=[SMEM] * 3 + [VMEM],
+        in_specs=[SMEM, VMEM],
         out_specs=VMEM,
         scratch_shapes=[
+            pltpu.SMEM(angles.shape, F32),
             pltpu.VMEM((lines * depth, width), F32),
-            pltpu.VMEM((depth // 2, lines, 2 * width), BF16),
+            pltpu.VMEM((depth // 4, 2 * lines, 2 * width), BF16),
             pltpu.VMEM((groups, 2, boxes, slab, width), BF16),
             pltpu.SemaphoreType.DMA((groups,)),
             pltpu.SemaphoreType.DMA((groups,)),
         ],
         compiler_params=pltpu.CompilerParams(
-            collective_id=0, has_side_effects=True, vmem_limit_bytes=32 * MIB
+            collective_id=0, has_side_effects=True, vmem_limit_bytes=20 * MIB
         ),
-    )(*tables, volumes.reshape(lines * depth, width))
+    )(angles, volumes.reshape(lines * depth, width))
 
 
 def call_place(windows, rows, cols, strips):
@@ -447,11 +546,11 @@
         in_specs=[SMEM, SMEM, VMEM],
         out_specs=VMEM,
         scratch_shapes=[pltpu.VMEM((2, (strips + 1) * 128 + 128, 256), F32)],
-        compiler_params=pltpu.CompilerParams(vmem_limit_bytes=40 * MIB),
+        compiler_params=pltpu.CompilerParams(vmem_limit_bytes=20 * MIB),
     )(rows, cols, windows)
 
 
-def call_image(canvas, spread, measured):
+def call_image(canvas, defocus, measured):
     dma = lambda *shape: pltpu.SemaphoreType.DMA(shape)
     blocks = lambda *shape: pltpu.VMEM(shape, BF16)
     return pl.pallas_call(
@@ -463,6 +562,8 @@
         in_specs=[SMEM, VMEM, VMEM],
         out_specs=(VMEM, VMEM),
         scratch_shapes=[
+            pltpu.VMEM((2, 16, 128), F32),
+            pltpu.SMEM((2, 16, 128), F32),
             blocks(2, 4, 4, 128, 256),
             blocks(2, 3, 4, 128, 256),
             blocks(2, 2, 2, 128, 256),
@@ -480,81 +581,59 @@
             dma(2, 2, 4),
             dma(2, 2, 6),
             dma(2, 2, 6),
-            dma(2, 4),
+            dma(2, 5),
             dma(2, 2, 36),
         ],
         compiler_params=pltpu.CompilerParams(
-            collective_id=1, has_side_effects=True, vmem_limit_bytes=48 * MIB
+            collective_id=1, has_side_effects=True, vmem_limit_bytes=24 * MIB
         ),
-    )(spread, canvas.reshape(2, 4, 4, 2, 128, 256), measured)
+    )(defocus, canvas.reshape(2, 4, 4, 2, 128, 256), measured)
 
 
 def call_cut(image, rows, cols):
-    boxes, tilts = rows.shape
+    tilts, boxes = rows.shape
     return pl.pallas_call(
         cut_kernel,
         out_shape=jax.ShapeDtypeStruct((tilts, boxes, 128, 128), BF16),
         in_specs=[SMEM, SMEM, VMEM],
         out_specs=VMEM,
         scratch_shapes=[pltpu.VMEM((tilts * boxes, 272, 256), F32)],
-        compiler_params=pltpu.CompilerParams(vmem_limit_bytes=32 * MIB),
+        compiler_params=pltpu.CompilerParams(vmem_limit_bytes=16 * MIB),
     )(rows, cols, image.reshape(2, 4096, 256))
 
 
-def call_exchange(windows, groups):
-    tilts, boxes = windows.shape[:2]
-    return pl.pallas_call(
-        functools.partial(exchange_kernel, groups),
-        out_shape=jax.ShapeDtypeStruct((groups, tilts, boxes, 16, 128), BF16),
-        in_specs=[VMEM],
-        out_specs=VMEM,
-        scratch_shapes=[pltpu.SemaphoreType.DMA((7,)), pltpu.SemaphoreType.DMA((7,))],
-        compiler_params=pltpu.CompilerParams(
-            collective_id=2, has_side_effects=True, vmem_limit_bytes=32 * MIB
-        ),
-    )(windows)
-
-
-def call_back(back_rows, tables, shape):
+def call_back(windows, angles, shape, groups):
     boxes, slab, depth, width = shape
     lines = boxes * slab
-    tilts = back_rows.shape[0] * 2
-    per_step = 8
     return pl.pallas_call(
-        functools.partial(back_kernel, 1.0 / tilts),
-        grid=(depth // per_step,),
+        functools.partial(back_kernel, groups, 1.0 / (2 * groups)),
         out_shape=jax.ShapeDtypeStruct((lines, depth, width), F32),
-        in_specs=[SMEM] * 3 + [pl.BlockSpec((tilts, lines, width), lambda i: (0, 0, 0))],
-        out_specs=pl.BlockSpec((lines, per_step, width), lambda i: (0, i, 0)),
-        scratch_shapes=[pltpu.VMEM((tilts // 2, lines, 2 * width), BF16)],
-        compiler_params=pltpu.CompilerParams(vmem_limit_bytes=32 * MIB),
-    )(*tables, back_rows.reshape(tilts, lines, width)).reshape(shape)
-
-
-def shear_tables(angles, depth):
-    layers = jnp.arange(depth, dtype=F32)
-    shift = (layers - (depth - 1) / 2.0) * jnp.sin(angles)[:, None]
-    tap = jnp.floor(shift)
-    weight = lambda offset: jnp.maximum(0.0, 1.0 - jnp.abs(offset - shift)).astype(BF16).astype(F32)
-    return tap, weight(tap), weight(tap + 1.0)
-
-
-def spread_table(defocus):
-    steps = jnp.arange(HR + 1, dtype=F32)
-    rho_sq = (steps[:, None] ** 2 + steps[None, :] ** 2).reshape(1, -1)
-    scale = float(HR * HR)
-    values = jnp.exp(-rho_sq / (2.0 * scale)) * jnp.cos(defocus[:, None] * rho_sq) / scale
-    return values.astype(BF16).astype(F32)
+        in_specs=[SMEM, VMEM],
+        out_specs=pl.BlockSpec(memory_space=pl.ANY),
+        scratch_shapes=[
+            pltpu.SMEM(angles.shape, F32),
+            pltpu.VMEM((groups, 2, boxes, slab, width), BF16),
+            pltpu.VMEM((2, 2 * lines, 2 * width), BF16),
+            pltpu.VMEM((16, 2 * lines, 2 * width), F32),
+            pltpu.VMEM((2, 4, lines, 8, width), F32),
+            pltpu.SemaphoreType.DMA((groups,)),
+            pltpu.SemaphoreType.DMA((groups,)),
+            pltpu.SemaphoreType.DMA((2, 4)),
+        ],
+        compiler_params=pltpu.CompilerParams(
+            collective_id=2, has_side_effects=True, vmem_limit_bytes=20 * MIB
+        ),
+    )(angles, windows).reshape(shape)
 
 
 def shards(volumes, angles, defocus, row_offsets, col_offsets, measured):
     groups = lax.axis_size("tilt")
-    tables = shear_tables(angles, volumes.shape[2])
-    windows = call_project(volumes, tables, groups)
-    canvas = call_place(windows, row_offsets, col_offsets, lax.axis_size("tile"))
-    residual, image = call_image(canvas, spread_table(defocus), measured)
-    back_rows = call_exchange(call_cut(image, row_offsets, col_offsets), groups)
-    return residual, call_back(back_rows, tables, volumes.shape)
+    windows = call_project(volumes, angles, groups)
+    rows, cols = row_offsets.T, col_offsets.T
+    canvas = call_place(windows, rows, cols, lax.axis_size("tile"))
+    residual, image = call_image(canvas, defocus, measured)
+    back_windows = call_cut(image, rows, cols)
+    return residual, call_back(back_windows, angles, volumes.shape, groups)
 
 
 def solution(mesh):

time: 138 us -> 101 us (0.73)
  Pallas kernels: 130 us -> 94.1 us
    pallas_call x2 -> x1, Pallas kernels: 43.3 us -> 22.2 us  [call_back(): pl.pallas_call(functools.partial(back_kernel, groups, 1.0 / (2 * groups))...]
    pallas_call x1, Pallas kernels: 33.7 us -> 20.9 us  [call_project(): pl.pallas_call(functools.partial(project_kernel, groups), out_shape=jax.S...]
    pallas_call x1, Pallas kernels: 48.7 us -> 47.2 us  [call_image(): pl.pallas_call(image_kernel, out_shape=(jax.ShapeDtypeStruct((2, 128, 256...]
    unnamed x9 -> x20, local copies, waits for them, and re-layouts: 5.58 us -> 5.8 us
where the time goes in v2:
time: 101 us
  Pallas kernels  94.1 us (93%)
  local copies, waits for them, and re-layouts  5.8 us (6%)
    pallas_call x1, Pallas kernels, call_image(): pl.pallas_call(image_kernel, out_shape=(jax.ShapeDtypeStruct((2, 128, 256...  47.2 us
    pallas_call x1, Pallas kernels, call_back(): pl.pallas_call(functools.partial(back_kernel, groups, 1.0 / (2 * groups))...  22.2 us
    pallas_call x1, Pallas kernels, call_project(): pl.pallas_call(functools.partial(project_kernel, groups), out_shape=jax.S...  20.9 us
    unnamed x20, local copies, waits for them, and re-layouts  5.8 us
    pallas_call x1, Pallas kernels, call_place(): pl.pallas_call(place_kernel, out_shape=jax.ShapeDtypeStruct((2, strips, 1...  2.5 us

profile of v2, /device:TPU:2, one launch (start us, length us, event | category | flops | bytes accessed | tf_op | source)
XLA Modules:
  0.0 100.7 jit_solution(10724187517258870982)
XLA Ops:
  0.6 0.0 copy-start
  0.6 1.4 %copy-done = bf16[6,16,64,128]{3,2,1,0:T(8,128)(2,1)S(1)} copy-done((bf16[6,16,64,128]{3,2,1,0:T(8,128)(2,1)S(1)}, bf16[6,16,64,128]{3,2,1,0:T(8,128)(2,1)}, u32[]{:S(2)}) %copy-start) | copy-done | bytes 1572888
  2.0 0.0 copy-start.6
  2.0 0.7 copy-done.6
  2.7 0.0 copy-start.1
  2.7 0.0 copy-start.8
  2.7 20.9 %shard_map.77.w_ref = bf16[2,6,128,128]{3,2,1,0:T(8,128)(2,1)S(1)} custom-call(f32[16]{0:T(128)S(1)} %copy-done.6, bf16[6144,128]{1,0:T(8,128)(2,1)S(1)} %bitcast.9), custom_call_target="tpu_custom_call" | custom-call | tf_op jit(solution)/shard_map/pallas_call | solution.py:523
  23.6 0.0 copy-start.2
  23.6 0.7 copy-done.2
  24.3 0.0 copy-start.4
  24.3 0.7 copy-done.4
  24.9 2.5 %shard_map.78 = bf16[2,32,128,256]{3,2,1,0:T(8,128)(2,1)S(1)} custom-call(s32[2,6]{1,0:T(2,128)S(1)} %bitcast.10, s32[2,6]{1,0:T(2,128)S(1)} %bitcast.12, bf16[2,6,128,128]{3,2,1,0:T(8,128)(2,1)S(1)} %shard_map.77.w_ref), custom_call_target="tpu_custom_call" | custom-call | tf_op jit(solution)/shard_map/pallas_call | solution.py:543
  27.4 0.0 copy-start.3
  27.5 0.0 copy-start.5
  27.5 0.0 copy-done.1
  27.5 0.0 copy-done.8
  27.5 47.2 %shard_map.79 = (f32[2,128,256]{2,1,0:T(8,128)S(1)}, bf16[2,4,4,2,128,256]{5,4,3,2,1,0:T(8,128)(2,1)S(1)}) custom-call(f32[2]{0:T(128)S(1)} %copy-done.8, bf16[2,4,4,2,128,256]{5,4,3,2,1,0:T(8,128)(2,1)S(1)} %bitcast.6, f32[2,128,256]{2,1,0:T(8,128)S(1)} %copy-done.1), custom_call_target="tpu_custom_call" | custom-call | tf_op jit(solution)/shard_map/pallas_call | solution.py:556
  74.7 0.0 copy-start.7
  74.7 0.0 copy-done.3
  74.7 0.0 copy-done.5
  74.7 1.4 %shard_map.80.windows = bf16[2,6,128,128]{3,2,1,0:T(8,128)(2,1)S(1)} custom-call(s32[2,6]{1,0:T(2,128)S(1)} %bitcast.11, s32[2,6]{1,0:T(2,128)S(1)} %bitcast.13, bf16[2,4096,256]{2,1,0:T(8,128)(2,1)S(1)} %bitcast.8), custom_call_target="tpu_custom_call" | custom-call | tf_op jit(solution)/shard_map/pallas_call | solution.py:595
  76.1 0.0 copy-done.7
  76.1 22.2 %shard_map.81 = f32[96,64,128]{2,1,0:T(8,128)S(1)} custom-call(f32[16]{0:T(128)S(1)} %copy-done.7, bf16[2,6,128,128]{3,2,1,0:T(8,128)(2,1)S(1)} %shard_map.80.windows), custom_call_target="tpu_custom_call" | custom-call | tf_op jit(solution)/shard_map/pallas_call | solution.py:608
  98.3 0.7 copy.10
  99.0 1.7 %copy.11 = f32[6,16,64,128]{3,2,1,0:T(8,128)} copy(f32[6,16,64,128]{3,2,1,0:T(8,128)S(1)} %bitcast.7) | data formatting | bytes 6291456
Async XLA Ops:
  0.6 1.4 %copy-start = (bf16[6,16,64,128]{3,2,1,0:T(8,128)(2,1)S(1)}, bf16[6,16,64,128]{3,2,1,0:T(8,128)(2,1)}, u32[]{:S(2)}) copy-start(bf16[6,16,64,128]{3,2,1,0:T(8,128)(2,1)} %param.6) | copy-start | bytes 4718596
  2.0 0.7 copy-start.6
  2.7 24.8 %copy-start.1 = (f32[2,128,256]{2,1,0:T(8,128)S(1)}, f32[2,128,256]{2,1,0:T(8,128)}, u32[]{:S(2)}) copy-start(f32[2,128,256]{2,1,0:T(8,128)} %measured.1) | copy-start | bytes 786436
  2.7 24.8 %copy-start.8 = (f32[2]{0:T(128)S(1)}, f32[2]{0:T(128)}, u32[]{:S(2)}) copy-start(f32[2]{0:T(128)} %defocus.1) | copy-start | bytes 28
  23.6 0.7 copy-start.2
  24.3 0.7 copy-start.4
  27.4 47.3 %copy-start.3 = (s32[6,2]{0,1:T(2,128)S(1)}, s32[6,2]{0,1:T(2,128)}, u32[]{:S(2)}) copy-start(s32[6,2]{0,1:T(2,128)} %param.9) | copy-start | bytes 148
  27.5 47.3 %copy-start.5 = (s32[6,2]{0,1:T(2,128)S(1)}, s32[6,2]{0,1:T(2,128)}, u32[]{:S(2)}) copy-start(s32[6,2]{0,1:T(2,128)} %param.10) | copy-start | bytes 148
  74.7 1.4 %copy-start.7 = (f32[16]{0:T(128)S(1)}, f32[16]{0:T(128)}, u32[]{:S(2)}) copy-start(f32[16]{0:T(128)} %angles.3) | copy-start | bytes 196

commit v3 on v2

v3 whole, which is shorter than its diff:
```python
import functools

import jax
import jax.numpy as jnp
from jax import lax
from jax.experimental import pallas as pl
from jax.experimental.pallas import tpu as pltpu
from jax.sharding import PartitionSpec as P

HR = 8
MESH = pl.DeviceIdType.MESH
BF16 = jnp.bfloat16
F32 = jnp.float32
MIB = 1 << 20


def signal(device):
    pl.semaphore_signal(
        pltpu.get_barrier_semaphore(), inc=1, device_id=device, device_id_type=MESH
    )


def remote(src, dst, send_sem, recv_sem, device):
    return pltpu.make_async_remote_copy(
        src_ref=src, dst_ref=dst, send_sem=send_sem, recv_sem=recv_sem,
        device_id=device, device_id_type=MESH,
    )


def offsets_c_minus_x(transposed):
    rows = lax.broadcasted_iota(jnp.int32, (128, 128), 0)
    cols = lax.broadcasted_iota(jnp.int32, (128, 128), 1)
    return ((rows - cols) if transposed else (cols - rows)).astype(F32).astype(BF16)


def sine(x):
    square = x * x
    value = -1.0 / 39916800.0 + square * (1.0 / 6227020800.0)
    for factor in (1.0 / 362880.0, -1.0 / 5040.0, 1.0 / 120.0, -1.0 / 6.0):
        value = factor + square * value
    return x + x * (square * value)


def shear_block(sines, tilt, layer, apart):
    shift = (jnp.asarray(layer, jnp.int32).astype(F32) - 31.5) * sines[tilt]
    tap = shift.astype(jnp.int32).astype(F32)
    tap = jnp.where(tap > shift, tap - 1.0, tap)
    all_of = lambda value: jnp.full((128, 128), value, F32).astype(BF16)
    near = jnp.maximum(0.0, 1.0 - jnp.abs(tap - shift))
    far = jnp.maximum(0.0, 1.0 - jnp.abs(tap + 1.0 - shift))
    zero = jnp.zeros((128, 128), BF16)
    return jnp.where(apart == all_of(tap), all_of(near), jnp.where(apart == all_of(tap + 1.0), all_of(far), zero))


def shear_tile(sines, tilt, layer, apart, transposed):
    make = lambda t, z: shear_block(sines, tilt + t, layer + z, apart)
    if transposed:
        parts = [[make(t, z) for z in range(2)] for t in range(2)]
    else:
        parts = [[make(t, z) for t in range(2)] for z in range(2)]
    return jnp.concatenate([jnp.concatenate(row, axis=1) for row in parts], axis=0)


def flip_matrix():
    rows = lax.broadcasted_iota(jnp.int32, (128, 128), 0)
    cols = lax.broadcasted_iota(jnp.int32, (128, 128), 1)
    return jnp.where(rows + cols == 127, 1.0, 0.0).astype(BF16)


def flipped(x, flip):
    high = x.astype(BF16)
    low = (x - high.astype(F32)).astype(BF16)
    return jnp.dot(
        jnp.concatenate([high, low], axis=1), jnp.concatenate([flip, flip], axis=0), preferred_element_type=F32
    )


def project_part(
    groups, me, tile, sibling, loads, ready, sines, v_ref, out_ref, pair_ref,
    wide, pairs, sent, send_sems, recv_sems, pair_sems,
):
    rows = v_ref.shape[0]
    lines = rows // 64
    parts = len(loads)
    size = rows // parts

    def widen(i, carry):
        at = pl.ds(pl.multiple_of(i * 512, 512), 512)
        wide[at, :] = v_ref[at, :].astype(F32)
        return carry

    for i in range(parts):
        loads[i].wait()
        lax.fori_loop(i * size // 512, (i + 1) * size // 512, widen, 0)
    flip = flip_matrix()

    def gather(k, carry):
        layer = lambda z: wide[pl.ds(z, lines, stride=64), :]
        top = jnp.concatenate([layer(2 * k), layer(2 * k + 1)], axis=1).astype(BF16)
        mirror = jnp.concatenate([layer(63 - 2 * k), layer(62 - 2 * k)], axis=0).astype(BF16)
        mirror = jnp.dot(mirror, flip, preferred_element_type=F32).astype(BF16)
        pairs[k] = jnp.concatenate([top, jnp.concatenate([mirror[:lines], mirror[lines:]], axis=1)], axis=0)
        return carry

    lax.fori_loop(0, 16, gather, 0)
    ready()
    apart = offsets_c_minus_x(False)
    mine = pl.ds(pl.multiple_of(16 * me, 16), 16)

    def windows_of(target):
        acc = jnp.zeros((2 * lines, 256), F32)
        for k in range(16):
            acc = acc + jnp.dot(
                pairs[k], shear_tile(sines, 2 * target, 2 * k, apart, False), preferred_element_type=F32
            )
        mirror = flipped(jnp.concatenate([acc[lines:, :128], acc[lines:, 128:]], axis=0), flip)
        both = (acc[:lines, :128] + mirror[:lines], acc[:lines, 128:] + mirror[lines:])
        return [half.astype(BF16).reshape(lines // 16, 16, 128) for half in both]

    def copy_of(step):
        d = jnp.where(step % 2 == 0, 4 + step // 2, 4 - (step + 1) // 2)
        target = (me + d) % groups
        return target, remote(
            sent.at[step], out_ref.at[:, :, mine, :], send_sems.at[step], recv_sems.at[step], (target, tile)
        )

    def project(step, carry):
        target, copy = copy_of(step)
        both = windows_of(target)
        for t in range(2):
            sent[step, t] = both[t]
        copy.start()
        return carry

    lax.fori_loop(0, groups - 1, project, 0)
    both = windows_of(me)
    for t in range(2):
        out_ref[t, :, mine, :] = both[t]

    def share(slab, k):
        at = pl.ds(pl.multiple_of(16 * slab, 16), 16)
        return remote(
            out_ref.at[:, :, at, :], pair_ref.at[:, :, at, :], pair_sems.at[0, k], pair_sems.at[1, k], sibling
        )

    def came_from(step):
        d = jnp.where(step % 2 == 0, 4 + step // 2, 4 - (step + 1) // 2)
        return (me + groups - d) % groups

    share(me, groups - 1).start()

    def forward(step, carry):
        copy_of(step)[1].wait_recv()
        share(came_from(step), step).start()
        return carry

    lax.fori_loop(0, groups - 1, forward, 0)

    def finish(step, carry):
        copy_of(step)[1].wait_send()
        share(came_from(step), step).wait()
        return carry

    lax.fori_loop(0, groups - 1, finish, 0)
    share(me, groups - 1).wait()


def ring_devices():
    z, tile = lax.axis_index("tilt"), lax.axis_index("tile")
    x, y, c = tile // 8, (tile // 2) % 4, tile % 2

    def dev(dx, dy):
        return (z, ((x + dx) % 4) * 8 + ((y + dy) % 4) * 2 + c)

    right = (dev(1, 0), dev(0, 1))
    left = (dev(3, 0), dev(0, 3))
    sibling = (z, x * 8 + y * 2 + 1 - c)
    return right, left, sibling, (z, (tile + 1) % 32), (z, (tile + 31) % 32)


def image_part(
    defocus, rows_a, cols_a, rows_b, cols_b, win_a, win_b, measured, residual, img, spread_wide, spread,
    shifted, select, loc, s_b, o_b, f_b, s_c, o_c, f_c, table, pred_half, pred, halo, m_halo, res,
    b_sems, c_sems, h_sems, g_sems,
):
    z, tile = lax.axis_index("tilt"), lax.axis_index("tile")
    x, y, c = tile // 8, (tile // 2) % 4, tile % 2
    rights, lefts, sibling, below, above = ring_devices()
    right = lambda axis: rights[axis]
    left = lambda axis: lefts[axis]
    place = (x, y)
    steps = (2, 1, 3, 0)
    m_copies = []
    for k, (device, start) in enumerate(((below, 120), (above, 0))):
        copy = remote(
            measured.at[:, pl.ds(start, 8), :], m_halo.at[k], h_sems.at[0, k], h_sems.at[1, k], device
        )
        copy.start()
        m_copies.append(copy)

    down = lax.broadcasted_iota(jnp.int32, (16, 128), 0).astype(F32)
    along = lax.broadcasted_iota(jnp.int32, (16, 128), 1).astype(F32)
    rho_sq = down * down + along * along
    scale = float(HR * HR)
    for t in range(2):
        spread_wide[t] = jnp.exp(-rho_sq / (2.0 * scale)) * jnp.cos(defocus[0, t] * rho_sq) / scale
    to_scalars = pltpu.make_async_copy(spread_wide, spread, h_sems.at[0, 4])
    to_scalars.start()

    def fill(i, carry):
        lanes = lax.broadcasted_iota(jnp.int32, (16, 256), 1)
        subs = lax.broadcasted_iota(jnp.int32, (16, 256), 0) + i * 16
        apart = jnp.abs(lanes - subs).astype(F32).astype(BF16)
        masks = [apart == jnp.full((16, 256), j, F32).astype(BF16) for j in range(HR + 1)]
        for t in range(2):
            for a in range(HR + 1):
                value = jnp.zeros((16, 256), BF16)
                for j in range(HR + 1):
                    value = jnp.where(masks[j], jnp.full((16, 256), spread[t, a, j], F32).astype(BF16), value)
                table[t, a, pl.ds(pl.multiple_of(i * 16, 16), 16), :] = value
        return carry


    pending = []

    def go(src, dst, sems, t, k, device):
        copy = remote(src, dst, sems.at[0, t, k], sems.at[1, t, k], device)
        copy.start()
        pending.append(copy)
        return copy

    def at_place(t, p, q):
        return (p, q) if t == 0 else (q, p)

    boxes = win_a.shape[1]
    items = [(win_a, rows_a, cols_a, i) for i in range(boxes)] + [(win_b, rows_b, cols_b, i) for i in range(boxes)]
    left_by = lax.broadcasted_iota(jnp.int32, (128, 256), 1) - lax.broadcasted_iota(jnp.int32, (128, 256), 0)
    left_by = left_by.astype(F32).astype(BF16)
    down_by = lax.broadcasted_iota(jnp.int32, (128, 128), 0) - lax.broadcasted_iota(jnp.int32, (128, 128), 1)
    down_by = down_by.astype(F32).astype(BF16)

    def shift_columns(t):
        for i, (windows, _, cols_ref, b) in enumerate(items):
            col = jnp.full((128, 256), cols_ref[t, b].astype(F32), F32).astype(BF16)
            onto = jnp.where(left_by == col, 1.0, 0.0).astype(BF16)
            moved = jnp.dot(windows[t, b], onto, preferred_element_type=F32)
            shifted[t, pl.ds(128 * i, 128), :] = moved.astype(BF16)

    def canvas(t, k):
        p = (place[t] + steps[k]) % 4
        for q in range(4):
            bx, by = at_place(t, p, q)
            top = (bx * 8 + by * 2 + c) * 128
            for i, (_, rows_ref, _, b) in enumerate(items):
                row = jnp.clip(rows_ref[t, b] - top, -128, 128)
                row = jnp.full((128, 128), row.astype(F32), F32).astype(BF16)
                select[t, pl.ds(128 * q, 128), pl.ds(128 * i, 128)] = jnp.where(down_by == row, 1.0, 0.0).astype(BF16)
        return jnp.dot(select[t], shifted[t], preferred_element_type=F32).reshape(4, 128, 256)

    b_in = {}
    for t in range(2):
        shift_columns(t)
        s_b[t, 0] = canvas(t, 0).astype(BF16)
        for h, device in ((0, right(t)), (1, left(t))):
            b_in[t, "opp", h] = go(s_b.at[t, 0, pl.ds(2 * h, 2)], o_b.at[t, h], b_sems, t, h, device)
    for t in range(2):
        for k, h, device in ((1, 1, right(t)), (2, 0, left(t))):
            loc[t, k - 1] = canvas(t, k)
            at = pl.ds(2 * h, 2)
            s_b[t, k, at] = loc[t, k - 1, at].astype(BF16)
            b_in[t, "free", k] = go(s_b.at[t, k, at], f_b.at[t, k - 1, at], b_sems, t, 1 + k, device)
    for t in range(2):
        for k, h, device in ((1, 0, right(t)), (2, 1, left(t))):
            at = pl.ds(2 * h, 2)
            b_in[t, "opp", h].wait_recv()
            s_b[t, k, at] = (loc[t, k - 1, at] + o_b[t, h].astype(F32)).astype(BF16)
            b_in[t, "bound", k] = go(s_b.at[t, k, at], f_b.at[t, k - 1, at], b_sems, t, 3 + k, device)
    for t in range(2):
        loc[t, 2] = canvas(t, 3)
    to_scalars.wait()
    lax.fori_loop(0, 16, fill, 0)
    for t in range(2):
        for k in (1, 2):
            b_in[t, "free", k].wait_recv()
            b_in[t, "bound", k].wait_recv()

    def local_c(t, k, half):
        q = (place[1 - t] + steps[k]) % 4
        at = pl.ds(64 * half, 64)
        return loc[t, 2, q, at, :] + f_b[t, 0, q, at, :].astype(F32) + f_b[t, 1, q, at, :].astype(F32)

    c_in = {}
    for t in range(2):
        for h, device in ((0, right(1 - t)), (1, left(1 - t))):
            at = pl.ds(64 * h, 64)
            s_c[t, 0, at] = local_c(t, 0, h).astype(BF16)
            c_in[t, "opp", h] = go(s_c.at[t, 0, at], o_c.at[t, h], c_sems, t, h, device)
        for k, h, device in ((1, 1, right(1 - t)), (2, 0, left(1 - t))):
            at = pl.ds(64 * h, 64)
            s_c[t, k, at] = local_c(t, k, h).astype(BF16)
            c_in[t, "free", k] = go(s_c.at[t, k, at], f_c.at[t, k - 1, at], c_sems, t, 1 + k, device)
    for t in range(2):
        for k, h, device in ((1, 0, right(1 - t)), (2, 1, left(1 - t))):
            at = pl.ds(64 * h, 64)
            c_in[t, "opp", h].wait_recv()
            s_c[t, k, at] = (local_c(t, k, h) + o_c[t, h].astype(F32)).astype(BF16)
            c_in[t, "bound", k] = go(s_c.at[t, k, at], f_c.at[t, k - 1, at], c_sems, t, 3 + k, device)
    for t in range(2):
        for k in (1, 2):
            c_in[t, "free", k].wait_recv()
            c_in[t, "bound", k].wait_recv()
        total = jnp.concatenate([local_c(t, 3, h) for h in range(2)], axis=0)
        total = total + f_c[t, 0].astype(F32) + f_c[t, 1].astype(F32)
        pred_half[t] = total.astype(BF16)
        pred[t, pl.ds(16, 128), :] = pred_half[t].astype(F32)

    p_copies = []
    for k, (device, start) in enumerate(((below, 112), (above, 0))):
        copy = remote(
            pred_half.at[:, pl.ds(start, 16), :], halo.at[k], h_sems.at[0, 2 + k], h_sems.at[1, 2 + k], device
        )
        copy.start()
        p_copies.append(copy)
    has_above = jnp.where(tile > 0, 1.0, 0.0).astype(F32)
    has_below = jnp.where(tile < 31, 1.0, 0.0).astype(F32)
    for copy in m_copies + p_copies:
        copy.wait_recv()
    for t in range(2):
        pred[t, pl.ds(0, 16), :] = halo[0, t].astype(F32) * has_above
        pred[t, pl.ds(144, 16), :] = halo[1, t].astype(F32) * has_below

    g_in = {}

    def give(t, bx, by, core, rows, k, device):
        top = (bx * 8 + by * 2 + core) * 128 + rows[0]
        where = img.at[t, pl.ds(pl.multiple_of(top, 64), rows[1]), :]
        copy = remote(where, where, g_sems.at[0, t, k], g_sems.at[1, t, k], device)
        copy.start()
        pending.append(copy)
        return copy

    for t in range(2):
        total = jnp.zeros((144, 256), F32)
        for i in range(2 * HR + 1):
            lhs = pred[t, pl.ds(i, 144), :].astype(BF16)
            total = total + jnp.dot(lhs, table[t, abs(i - HR)], preferred_element_type=F32)
        inner = measured[t] - total[8:136]
        residual[t] = inner
        res[t, pl.ds(8, 128), :] = inner.astype(BF16).astype(F32)
        res[t, pl.ds(0, 8), :] = (m_halo[0, t] - total[0:8]).astype(BF16).astype(F32) * has_above
        res[t, pl.ds(136, 8), :] = (m_halo[1, t] - total[136:144]).astype(BF16).astype(F32) * has_below
        total = jnp.zeros((128, 256), F32)
        for i in range(2 * HR + 1):
            lhs = res[t, pl.ds(i, 128), :].astype(BF16)
            total = total + jnp.dot(lhs, table[t, abs(i - HR)], preferred_element_type=F32)
        img[t, pl.ds(pl.multiple_of(tile * 128, 128), 128), :] = total.astype(BF16)
        whole = (0, 128)
        g_in[t, "q", 0] = give(t, x, y, c, whole, 0, right(1 - t))
        g_in[t, "q", 1] = give(t, x, y, c, whole, 1, left(1 - t))
        g_in[t, "p", 0, 0] = give(t, x, y, c, whole, 4, right(t))
        g_in[t, "p", 0, 1] = give(t, x, y, c, whole, 5, left(t))
        g_in[t, "s", 0, 0] = give(t, x, y, c, whole, 20, sibling)

    def spread_block(t, dq, slot):
        q = (place[1 - t] + dq) % 4
        bx, by = at_place(t, place[t], q)
        g_in[t, "p", slot, 0] = give(t, bx, by, c, (0, 128), 4 + 4 * slot, right(t))
        g_in[t, "p", slot, 1] = give(t, bx, by, c, (0, 128), 5 + 4 * slot, left(t))
        g_in[t, "s", 0, slot] = give(t, bx, by, c, (0, 128), 20 + slot, sibling)

    for t in range(2):
        g_in[t, "q", 0].wait_recv()
        bx, by = at_place(t, place[t], (place[1 - t] + 3) % 4)
        g_in[t, "q", 2] = give(t, bx, by, c, (0, 64), 2, right(1 - t))
        g_in[t, "q", 1].wait_recv()
        bx2, by2 = at_place(t, place[t], (place[1 - t] + 1) % 4)
        g_in[t, "q", 3] = give(t, bx2, by2, c, (64, 64), 3, left(1 - t))
        spread_block(t, 3, 1)
        spread_block(t, 1, 2)
    for t in range(2):
        g_in[t, "q", 2].wait_recv()
        g_in[t, "q", 3].wait_recv()
        spread_block(t, 2, 3)

    offsets = (0, 3, 1, 2)
    for slot in range(4):
        for t in range(2):
            q = (place[1 - t] + offsets[slot]) % 4
            for side, (dp, start, device) in enumerate(((3, 0, right(t)), (1, 64, left(t)))):
                g_in[t, "p", slot, side].wait_recv()
                bx, by = at_place(t, (place[t] + dp) % 4, q)
                g_in[t, "f", slot, side] = give(t, bx, by, c, (start, 64), 6 + 4 * slot + side, device)
                g_in[t, "s", 1 + side, slot] = give(t, bx, by, c, (0, 128), 24 + 4 * side + slot, sibling)
    for slot in range(4):
        for t in range(2):
            q = (place[1 - t] + offsets[slot]) % 4
            g_in[t, "f", slot, 0].wait_recv()
            g_in[t, "f", slot, 1].wait_recv()
            bx, by = at_place(t, (place[t] + 2) % 4, q)
            g_in[t, "s", 3, slot] = give(t, bx, by, c, (0, 128), 32 + slot, sibling)
    for slot in range(4):
        for t in range(2):
            for column in range(4):
                g_in[t, "s", column, slot].wait_recv()
    for copy in m_copies + p_copies + pending:
        copy.wait_send()


def cut_part(rows_ref, cols_ref, img, out_ref):
    tilts, boxes = out_ref.shape[:2]
    count = img.shape[1] // 128
    apart = lambda n, m: (
        lax.broadcasted_iota(jnp.int32, (n, m), 0) - lax.broadcasted_iota(jnp.int32, (n, m), 1)
    ).astype(F32).astype(BF16)
    down_by, left_by = apart(128, 256), apart(256, 128)
    fill = lambda value, n, m: jnp.full((n, m), value.astype(F32), F32).astype(BF16)
    for t in range(tilts):
        for b in range(boxes):
            row, col = rows_ref[t, b], cols_ref[t, b]
            home = row // 128
            first, second = fill(home, 128, 256), fill(home + 1, 128, 256)

            def choose(strip, both):
                block = img[t, pl.ds(pl.multiple_of(strip * 128, 128), 128), :]
                here = fill(strip, 128, 256)
                return jnp.where(first == here, block, both[0]), jnp.where(second == here, block, both[1])

            nothing = jnp.zeros((128, 256), BF16)
            rough = jnp.concatenate(lax.fori_loop(0, count, choose, (nothing, nothing), unroll=2), axis=0)
            pick = jnp.where(down_by == fill(home * 128 - row, 128, 256), 1.0, 0.0).astype(BF16)
            lines = jnp.dot(pick, rough, preferred_element_type=F32).astype(BF16)
            pick = jnp.where(left_by == fill(col, 256, 128), 1.0, 0.0).astype(BF16)
            out_ref[t, b] = jnp.dot(lines, pick, preferred_element_type=F32).astype(BF16)


ORDER = ((0, 1), (7, 2), (6, 3), (5, 4))


def layer_product(lines, sines, groups_of, layer, apart):
    acc = jnp.zeros((lines.shape[1], 256), F32)
    for slot in range(2):
        weights = shear_tile(sines, 2 * groups_of[slot], layer, apart, True)
        acc = acc + jnp.dot(lines[slot], weights, preferred_element_type=F32)
    return acc


def back_part(groups, me, tile, sines, windows, sums_hbm, lines_hbm, got, lines, sums, send_sems, recv_sems, sems):
    flip = flip_matrix()
    count = lines.shape[1] // 2
    copies = {}
    for d in (1, 7, 2, 6, 3, 5, 4):
        target = (me + d) % groups
        copies[d] = remote(
            windows.at[:, :, pl.ds(pl.multiple_of(16 * target, 16), 16), :], got.at[d],
            send_sems.at[d], recv_sems.at[d], (target, tile),
        )
        copies[d].start()
    apart = offsets_c_minus_x(True)

    def take(slot, rows):
        for t in range(2):
            at = pl.ds(128 * t, 128)
            line = rows[t].reshape(count, 128)
            lines[slot, pl.ds(0, count), at] = line
            lines[slot, pl.ds(count, count), at] = jnp.dot(line, flip, preferred_element_type=F32).astype(BF16)

    def out_copy(i):
        at = pl.ds(4 * i, 4)
        return pltpu.make_async_copy(sums.at[at], sums_hbm.at[at], sems.at[i])

    for stage, pair in enumerate(ORDER):
        for slot, d in enumerate(pair):
            if d == 0:
                take(slot, windows[:, :, pl.ds(pl.multiple_of(16 * me, 16), 16), :])
            else:
                copies[d].wait_recv()
                take(slot, got[d])
        if stage == 3:
            break
        from_group = [(me - d + groups) % groups for d in pair]

        def add(i, carry):
            for k in range(4):
                value = layer_product(lines, sines, from_group, 8 * i + 2 * k, apart)
                sums[4 * i + k] = value if stage == 0 else sums[4 * i + k] + value
            if stage == 2:
                out_copy(i).start()
            return carry

        lax.fori_loop(0, 4, add, 0)
    last = pltpu.make_async_copy(lines, lines_hbm, sems.at[4])
    last.start()

    def finish(i, carry):
        out_copy(i).wait()
        return carry

    lax.fori_loop(0, 4, finish, 0)
    last.wait()
    for copy in copies.values():
        copy.wait_send()


def finish_kernel(
    groups, angles_hbm, lines_hbm, sums_hbm, residual_hbm, residual, out_ref,
    angles, sines, lines, sums, blocks, load_sems, sems,
):
    me = lax.axis_index("tilt")

    def sums_copy(i):
        at = pl.ds(4 * i, 4)
        return pltpu.make_async_copy(sums_hbm.at[at], sums.at[at], load_sems.at[i])

    smalls = [
        pltpu.make_async_copy(src, dst, load_sems.at[4 + k])
        for k, (src, dst) in enumerate(((angles_hbm, angles), (lines_hbm, lines), (residual_hbm, residual)))
    ]
    smalls[0].start()
    smalls[1].start()
    for i in range(4):
        sums_copy(i).start()
    smalls[2].start()
    smalls[0].wait()
    for t in range(sines.shape[0]):
        sines[t] = sine(angles[0, t])
    smalls[1].wait()
    flip = flip_matrix()
    apart = offsets_c_minus_x(True)
    count = lines.shape[1] // 2
    scale = 1.0 / (2 * groups)
    from_group = [(me - d + groups) % groups for d in ORDER[-1]]

    def copies_of(i):
        low = pltpu.make_async_copy(
            blocks.at[0, i], out_ref.at[:, pl.ds(pl.multiple_of(8 * i, 8), 8), :], sems.at[0, i]
        )
        high = pltpu.make_async_copy(
            blocks.at[1, i], out_ref.at[:, pl.ds(pl.multiple_of(56 - 8 * i, 8), 8), :], sems.at[1, i]
        )
        return low, high

    def layers(i, carry):
        sums_copy(i).wait()
        for k in range(4):
            acc = (sums[4 * i + k] + layer_product(lines, sines, from_group, 8 * i + 2 * k, apart)) * scale
            blocks[0, i, :, 2 * k, :] = acc[:count, :128]
            blocks[0, i, :, 2 * k + 1, :] = acc[:count, 128:]
            mirror = flipped(jnp.concatenate([acc[count:, :128], acc[count:, 128:]], axis=0), flip)
            blocks[1, i, :, 7 - 2 * k, :] = mirror[:count]
            blocks[1, i, :, 6 - 2 * k, :] = mirror[count:]
        for copy in copies_of(i):
            copy.start()
        return carry

    lax.fori_loop(0, 4, layers, 0)

    def finish(i, carry):
        for copy in copies_of(i):
            copy.wait()
        return carry

    lax.fori_loop(0, 4, finish, 0)
    smalls[2].wait()


def whole_kernel(
    groups, angles_hbm, rows_hbm, cols_hbm, defocus_hbm, v_hbm, m_hbm, residual_hbm, sums_hbm, lines_hbm,
    angles, sines, rows, cols, defocus, rows_b, cols_b, rows_v, cols_v, rows_bv, cols_bv, v_ref, measured,
    residual, windows, windows_b, img, back_windows, load_sems, v_sems, note_sems, *rest
):
    project_refs, image_refs, back_refs = rest[:6], rest[6:-6], rest[-6:]
    me, tile = lax.axis_index("tilt"), lax.axis_index("tile")
    rights, lefts, sibling, below, above = ring_devices()
    smalls = [
        pltpu.make_async_copy(src, dst, load_sems.at[k])
        for k, (src, dst) in enumerate((
            (angles_hbm, angles), (rows_hbm, rows_v), (cols_hbm, cols_v), (rows_hbm, rows), (cols_hbm, cols),
            (defocus_hbm, defocus), (m_hbm, measured),
        ))
    ]
    parts = v_sems.shape[0]
    size = v_ref.shape[0] // parts
    loads = []
    for i in range(parts):
        at = pl.ds(i * size, size)
        loads.append(pltpu.make_async_copy(v_hbm.at[at], v_ref.at[at], v_sems.at[i]))
        loads[-1].start()
    for copy in smalls:
        copy.start()
    partners = [((me + d) % groups, tile) for d in range(1, groups)]
    partners += [sibling, below, above, rights[0], rights[1], lefts[0], lefts[1]]
    for device in partners:
        signal(device)
    smalls[0].wait()
    for t in range(sines.shape[0]):
        sines[t] = sine(angles[0, t])
    notes = [
        remote(src, dst, note_sems.at[0, k], note_sems.at[1, k], sibling)
        for k, (src, dst) in enumerate(((rows_v, rows_bv), (cols_v, cols_bv)))
    ]

    def ready():
        pl.semaphore_wait(pltpu.get_barrier_semaphore(), len(partners))
        for k in (1, 2):
            smalls[k].wait()
        for copy in notes:
            copy.start()

    project_part(groups, me, tile, sibling, loads, ready, sines, v_ref, windows, windows_b, *project_refs)
    for copy in notes:
        copy.wait()
    into = [
        pltpu.make_async_copy(src, dst, load_sems.at[7 + k])
        for k, (src, dst) in enumerate(((rows_bv, rows_b), (cols_bv, cols_b)))
    ]
    for copy in into:
        copy.start()
    for copy in smalls[3:] + into:
        copy.wait()
    image_part(defocus, rows, cols, rows_b, cols_b, windows, windows_b, measured, residual, img, *image_refs)
    keep = pltpu.make_async_copy(residual, residual_hbm, load_sems.at[9])
    keep.start()
    cut_part(rows, cols, img, back_windows)
    back_part(groups, me, tile, sines, back_windows, sums_hbm, lines_hbm, *back_refs)
    keep.wait()


VMEM = pl.BlockSpec(memory_space=pltpu.VMEM)
HBM = pl.BlockSpec(memory_space=pltpu.HBM)


def call_whole(volumes, angles, defocus, rows, cols, measured, groups):
    boxes, slab, depth, width = volumes.shape
    lines = boxes * slab
    dma = lambda *shape: pltpu.SemaphoreType.DMA(shape)
    blocks = lambda *shape: pltpu.VMEM(shape, BF16)
    floats = lambda *shape: pltpu.VMEM(shape, F32)
    count = 2 * boxes * 128
    whole = [
        pltpu.SMEM((1, 2 * groups), F32),
        pltpu.SMEM((2 * groups,), F32),
        pltpu.SMEM((2, boxes), jnp.int32),
        pltpu.SMEM((2, boxes), jnp.int32),
        pltpu.SMEM((1, 2), F32),
        pltpu.SMEM((2, boxes), jnp.int32),
        pltpu.SMEM((2, boxes), jnp.int32),
        pltpu.VMEM((2, boxes), jnp.int32),
        pltpu.VMEM((2, boxes), jnp.int32),
        pltpu.VMEM((2, boxes), jnp.int32),
        pltpu.VMEM((2, boxes), jnp.int32),
        blocks(lines * depth, width),
        floats(*measured.shape),
        floats(*measured.shape),
        blocks(2, boxes, slab * groups, width),
        blocks(2, boxes, slab * groups, width),
        blocks(2, 4096, 256),
        blocks(2, boxes, slab * groups, width),
        dma(10), dma(4), dma(2, 2),
    ]
    project = [
        floats(lines * depth, width),
        blocks(depth // 4, 2 * lines, 2 * width),
        blocks(groups, 2, boxes, slab, width),
        dma(groups), dma(groups), dma(2, groups),
    ]
    image = [
        floats(2, 16, 128),
        pltpu.SMEM((2, 16, 128), F32),
        blocks(2, count, 256),
        blocks(2, 512, count),
        floats(2, 3, 4, 128, 256),
        blocks(2, 3, 4, 128, 256),
        blocks(2, 2, 2, 128, 256),
        blocks(2, 2, 4, 128, 256),
        blocks(2, 3, 128, 256),
        blocks(2, 2, 64, 256),
        blocks(2, 2, 128, 256),
        blocks(2, 9, 256, 256),
        blocks(2, 128, 256),
        floats(2, 160, 256),
        blocks(2, 2, 16, 256),
        floats(2, 2, 8, 256),
        floats(2, 144, 256),
        dma(2, 2, 6), dma(2, 2, 6), dma(2, 5), dma(2, 2, 36),
    ]
    back = [
        blocks(groups, 2, boxes, slab, width),
        blocks(2, 2 * lines, 2 * width),
        floats(16, 2 * lines, 2 * width),
        dma(groups), dma(groups), dma(5),
    ]
    angles = angles.reshape(1, -1)
    residual, sums, last = pl.pallas_call(
        functools.partial(whole_kernel, groups),
        out_shape=(
            jax.ShapeDtypeStruct(measured.shape, F32),
            jax.ShapeDtypeStruct((16, 2 * lines, 2 * width), F32),
            jax.ShapeDtypeStruct((2, 2 * lines, 2 * width), BF16),
        ),
        in_specs=[HBM] * 6,
        out_specs=(HBM,) * 3,
        scratch_shapes=whole + project + image + back,
        compiler_params=pltpu.CompilerParams(
            collective_id=0, has_side_effects=True, vmem_limit_bytes=56 * MIB
        ),
    )(angles, rows, cols, defocus.reshape(1, -1), volumes.reshape(lines * depth, width), measured)
    residual, step = pl.pallas_call(
        functools.partial(finish_kernel, groups),
        out_shape=(
            jax.ShapeDtypeStruct(measured.shape, F32), jax.ShapeDtypeStruct((lines, depth, width), F32)
        ),
        in_specs=[HBM] * 4,
        out_specs=(HBM,) * 2,
        scratch_shapes=[
            pltpu.SMEM((1, 2 * groups), F32),
            pltpu.SMEM((2 * groups,), F32),
            blocks(2, 2 * lines, 2 * width),
            floats(16, 2 * lines, 2 * width),
            floats(2, 4, lines, 8, width),
            dma(7), dma(2, 4),
        ],
        compiler_params=pltpu.CompilerParams(vmem_limit_bytes=56 * MIB),
    )(angles, last, sums, residual)
    return residual, step.reshape(volumes.shape)


def shards(volumes, angles, defocus, row_offsets, col_offsets, measured):
    return call_whole(
        volumes, angles, defocus, row_offsets.T, col_offsets.T, measured, lax.axis_size("tilt")
    )


def solution(mesh):
    in_specs = (
        P("tile", "tilt", None, None),
        P(),
        P("tilt"),
        P("tile", "tilt"),
        P("tile", "tilt"),
        P("tilt", "tile", None),
    )
    out_specs = (P("tilt", "tile", None), P("tile", "tilt", None, None))
    return jax.shard_map(shards, mesh=mesh, in_specs=in_specs, out_specs=out_specs, check_vma=False)
```

time: 101 us -> 101 us (level)
  local copies, waits for them, and re-layouts: 5.8 us -> 0 us
  Pallas kernels: 94.1 us -> 99.2 us
    unnamed x20 -> x0, local copies, waits for them, and re-layouts: 5.8 us -> none
    pallas_call x5 -> x2, Pallas kernels: 94.1 us -> 99.2 us  [the longest x1 90 us: call_whole(): pl.pallas_call(functools.partial(whole_kernel, groups), out_shape=(jax.Sh...]
where the time goes in v3:
time: 101 us; the launch traced here: 100 us
  Pallas kernels  99.2 us (98%)
    pallas_call x1, Pallas kernels, call_whole(): pl.pallas_call(functools.partial(whole_kernel, groups), out_shape=(jax.Sh...  90 us
    pallas_call x1, Pallas kernels, call_whole(): pl.pallas_call(functools.partial(finish_kernel, groups), out_shape=(jax.S...  9.19 us

profile of v3, /device:TPU:2, one launch (start us, length us, event | category | flops | bytes accessed | tf_op | source)
XLA Modules:
  0.0 100.0 jit_solution(7029543728350855523)
XLA Ops:
  0.6 90.0 %shard_map.77 = (f32[2,128,256]{2,1,0:T(8,128)}, f32[16,192,256]{2,1,0:T(8,128)}, bf16[2,192,256]{2,1,0:T(8,128)(2,1)}) custom-call(f32[1,16]{1,0:T(1,128)} %bitcast.7, s32[2,6]{1,0:T(2,128)} %bitcast.9, s32[2,6]{1,0:T(2,128)} %bitcast.10, f32[1,2]{1,0:T(1,128)} %bitcast.11, bf16[6144,128]{1,0:T(8,128)(2,1)} %bitcast.6, f32[2,128,256]{2,1,0:T(8,128)} %m_hbm.1), custom_call_target="tpu_custom_call" | custom-call | tf_op jit(solution)/shard_map/pallas_call | solution.py:693
  90.7 9.2 %shard_map.78 = (f32[2,128,256]{2,1,0:T(8,128)}, f32[96,64,128]{2,1,0:T(8,128)}) custom-call(f32[1,16]{1,0:T(1,128)} %bitcast.8, bf16[2,192,256]{2,1,0:T(8,128)(2,1)} %get-tuple-element.7.lines_hbm, f32[16,192,256]{2,1,0:T(8,128)} %get-tuple-element.8.sums_hbm, f32[2,128,256]{2,1,0:T(8,128)} %get-tuple-element.9.residual_hbm), custom_call_target="tpu_custom_call" | custom-call | tf_op jit(solution)/shard_map/pallas_call | solution.py:707

commit v4 on v3

--- a/solution.py
+++ b/solution.py
@@ -406,7 +406,7 @@
         copy.wait_send()
 
 
-def cut_part(rows_ref, cols_ref, img, out_ref):
+def cut_part(rows_ref, cols_ref, img, out_ref, send):
     tilts, boxes = out_ref.shape[:2]
     count = img.shape[1] // 128
     apart = lambda n, m: (
@@ -418,19 +418,21 @@
         for b in range(boxes):
             row, col = rows_ref[t, b], cols_ref[t, b]
             home = row // 128
-            first, second = fill(home, 128, 256), fill(home + 1, 128, 256)
+            first, second = fill(home, 16, 256), fill(home + 1, 16, 256)
 
             def choose(strip, both):
-                block = img[t, pl.ds(pl.multiple_of(strip * 128, 128), 128), :]
-                here = fill(strip, 128, 256)
-                return jnp.where(first == here, block, both[0]), jnp.where(second == here, block, both[1])
-
-            nothing = jnp.zeros((128, 256), BF16)
-            rough = jnp.concatenate(lax.fori_loop(0, count, choose, (nothing, nothing), unroll=2), axis=0)
+                here = fill(strip, 16, 256)
+                masks = [first == here] * 8 + [second == here] * 8
+                block = [img[t, pl.ds(pl.multiple_of(strip * 128 + 16 * k, 16), 16), :] for k in range(8)] * 2
+                return tuple(jnp.where(*three) for three in zip(masks, block, both))
+
+            nothing = (jnp.zeros((16, 256), BF16),) * 16
+            rough = jnp.concatenate(lax.fori_loop(0, count, choose, nothing, unroll=2), axis=0)
             pick = jnp.where(down_by == fill(home * 128 - row, 128, 256), 1.0, 0.0).astype(BF16)
             lines = jnp.dot(pick, rough, preferred_element_type=F32).astype(BF16)
             pick = jnp.where(left_by == fill(col, 256, 128), 1.0, 0.0).astype(BF16)
             out_ref[t, b] = jnp.dot(lines, pick, preferred_element_type=F32).astype(BF16)
+        send(t)
 
 
 ORDER = ((0, 1), (7, 2), (6, 3), (5, 4))
@@ -444,17 +446,21 @@
     return acc
 
 
-def back_part(groups, me, tile, sines, windows, sums_hbm, lines_hbm, got, lines, sums, send_sems, recv_sems, sems):
-    flip = flip_matrix()
-    count = lines.shape[1] // 2
+def back_copies(groups, me, tile, windows, got, send_sems, recv_sems):
     copies = {}
     for d in (1, 7, 2, 6, 3, 5, 4):
         target = (me + d) % groups
-        copies[d] = remote(
-            windows.at[:, :, pl.ds(pl.multiple_of(16 * target, 16), 16), :], got.at[d],
-            send_sems.at[d], recv_sems.at[d], (target, tile),
-        )
-        copies[d].start()
+        for t in range(2):
+            copies[t, d] = remote(
+                windows.at[t, :, pl.ds(pl.multiple_of(16 * target, 16), 16), :], got.at[d, t],
+                send_sems.at[t, d], recv_sems.at[t, d], (target, tile),
+            )
+    return copies
+
+
+def back_part(groups, me, sines, copies, windows, sums_hbm, lines_hbm, got, lines, sums, sems):
+    flip = flip_matrix()
+    count = lines.shape[1] // 2
     apart = offsets_c_minus_x(True)
 
     def take(slot, rows):
@@ -473,7 +479,8 @@
             if d == 0:
                 take(slot, windows[:, :, pl.ds(pl.multiple_of(16 * me, 16), 16), :])
             else:
-                copies[d].wait_recv()
+                for t in range(2):
+                    copies[t, d].wait_recv()
                 take(slot, got[d])
         if stage == 3:
             break
@@ -620,8 +627,16 @@
     image_part(defocus, rows, cols, rows_b, cols_b, windows, windows_b, measured, residual, img, *image_refs)
     keep = pltpu.make_async_copy(residual, residual_hbm, load_sems.at[9])
     keep.start()
-    cut_part(rows, cols, img, back_windows)
-    back_part(groups, me, tile, sines, back_windows, sums_hbm, lines_hbm, *back_refs)
+    got, lines, sums, send_sems, recv_sems, sems = back_refs
+    copies = back_copies(groups, me, tile, back_windows, got, send_sems, recv_sems)
+
+    def send(t):
+        for (tilt, _), copy in copies.items():
+            if tilt == t:
+                copy.start()
+
+    cut_part(rows, cols, img, back_windows, send)
+    back_part(groups, me, sines, copies, back_windows, sums_hbm, lines_hbm, got, lines, sums, sems)
     keep.wait()
 
 
@@ -687,7 +702,7 @@
         blocks(groups, 2, boxes, slab, width),
         blocks(2, 2 * lines, 2 * width),
         floats(16, 2 * lines, 2 * width),
-        dma(groups), dma(groups), dma(5),
+        dma(2, groups), dma(2, groups), dma(5),
     ]
     angles = angles.reshape(1, -1)
     residual, sums, last = pl.pallas_call(

time: 101 us -> 99.6 us (0.986)
  no operation moved by 1% of the time
where the time goes in v4:
time: 99.6 us; the launch traced here: 99.1 us
  Pallas kernels  98.3 us (99%)
    pallas_call x1, Pallas kernels, call_whole(): pl.pallas_call(functools.partial(whole_kernel, groups), out_shape=(jax.Sh...  89.1 us
    pallas_call x1, Pallas kernels, call_whole(): pl.pallas_call(functools.partial(finish_kernel, groups), out_shape=(jax.S...  9.19 us

profile of v4, /device:TPU:2, one launch (start us, length us, event | category | flops | bytes accessed | tf_op | source)
XLA Modules:
  0.0 99.1 jit_solution(17273640234868389275)
XLA Ops:
  0.6 89.1 %shard_map.77 = (f32[2,128,256]{2,1,0:T(8,128)}, f32[16,192,256]{2,1,0:T(8,128)}, bf16[2,192,256]{2,1,0:T(8,128)(2,1)}) custom-call(f32[1,16]{1,0:T(1,128)} %bitcast.7, s32[2,6]{1,0:T(2,128)} %bitcast.9, s32[2,6]{1,0:T(2,128)} %bitcast.10, f32[1,2]{1,0:T(1,128)} %bitcast.11, bf16[6144,128]{1,0:T(8,128)(2,1)} %bitcast.6, f32[2,128,256]{2,1,0:T(8,128)} %m_hbm.1), custom_call_target="tpu_custom_call" | custom-call | tf_op jit(solution)/shard_map/pallas_call | solution.py:708
  89.7 9.2 %shard_map.78 = (f32[2,128,256]{2,1,0:T(8,128)}, f32[96,64,128]{2,1,0:T(8,128)}) custom-call(f32[1,16]{1,0:T(1,128)} %bitcast.8, bf16[2,192,256]{2,1,0:T(8,128)(2,1)} %get-tuple-element.7.lines_hbm, f32[16,192,256]{2,1,0:T(8,128)} %get-tuple-element.8.sums_hbm, f32[2,128,256]{2,1,0:T(8,128)} %get-tuple-element.9.residual_hbm), custom_call_target="tpu_custom_call" | custom-call | tf_op jit(solution)/shard_map/pallas_call | solution.py:722

commit v5 on v4

--- a/solution.py
+++ b/solution.py
@@ -510,7 +510,7 @@
 
 def finish_kernel(
     groups, angles_hbm, lines_hbm, sums_hbm, residual_hbm, residual, out_ref,
-    angles, sines, lines, sums, blocks, load_sems, sems,
+    angles, sines, lines, sums, blocks, held, load_sems, sems,
 ):
     me = lax.axis_index("tilt")
 
@@ -520,13 +520,14 @@
 
     smalls = [
         pltpu.make_async_copy(src, dst, load_sems.at[4 + k])
-        for k, (src, dst) in enumerate(((angles_hbm, angles), (lines_hbm, lines), (residual_hbm, residual)))
+        for k, (src, dst) in enumerate(((angles_hbm, angles), (lines_hbm, lines), (residual_hbm, held)))
     ]
     smalls[0].start()
     smalls[1].start()
+    smalls[2].start()
     for i in range(4):
         sums_copy(i).start()
-    smalls[2].start()
+    through = pltpu.make_async_copy(held, residual, load_sems.at[7])
     smalls[0].wait()
     for t in range(sines.shape[0]):
         sines[t] = sine(angles[0, t])
@@ -559,6 +560,8 @@
             copy.start()
         return carry
 
+    smalls[2].wait()
+    through.start()
     lax.fori_loop(0, 4, layers, 0)
 
     def finish(i, carry):
@@ -567,7 +570,7 @@
         return carry
 
     lax.fori_loop(0, 4, finish, 0)
-    smalls[2].wait()
+    through.wait()
 
 
 def whole_kernel(
@@ -732,7 +735,8 @@
             blocks(2, 2 * lines, 2 * width),
             floats(16, 2 * lines, 2 * width),
             floats(2, 4, lines, 8, width),
-            dma(7), dma(2, 4),
+            floats(*measured.shape),
+            dma(8), dma(2, 4),
         ],
         compiler_params=pltpu.CompilerParams(vmem_limit_bytes=56 * MIB),
     )(angles, last, sums, residual)

time: 99.6 us -> 97.5 us (0.979)
  Pallas kernels: 98.3 us -> 96.1 us
    pallas_call x1, Pallas kernels: 9.19 us -> 7.03 us  [call_whole(): pl.pallas_call(functools.partial(finish_kernel, groups), out_shape=(jax.S...]
where the time goes in v5:
time: 97.5 us; the launch traced here: 96.9 us
  Pallas kernels  96.1 us (99%)
    pallas_call x1, Pallas kernels, call_whole(): pl.pallas_call(functools.partial(whole_kernel, groups), out_shape=(jax.Sh...  89.1 us
    pallas_call x1, Pallas kernels, call_whole(): pl.pallas_call(functools.partial(finish_kernel, groups), out_shape=(jax.S...  7.03 us

profile of v5, /device:TPU:2, one launch (start us, length us, event | category | flops | bytes accessed | tf_op | source)
XLA Modules:
  0.0 96.9 jit_solution(12906680373983166105)
XLA Ops:
  0.6 89.1 %shard_map.77 = (f32[2,128,256]{2,1,0:T(8,128)}, f32[16,192,256]{2,1,0:T(8,128)}, bf16[2,192,256]{2,1,0:T(8,128)(2,1)}) custom-call(f32[1,16]{1,0:T(1,128)} %bitcast.7, s32[2,6]{1,0:T(2,128)} %bitcast.9, s32[2,6]{1,0:T(2,128)} %bitcast.10, f32[1,2]{1,0:T(1,128)} %bitcast.11, bf16[6144,128]{1,0:T(8,128)(2,1)} %bitcast.6, f32[2,128,256]{2,1,0:T(8,128)} %m_hbm.1), custom_call_target="tpu_custom_call" | custom-call | tf_op jit(solution)/shard_map/pallas_call | solution.py:711
  89.7 7.0 %shard_map.78 = (f32[2,128,256]{2,1,0:T(8,128)}, f32[96,64,128]{2,1,0:T(8,128)}) custom-call(f32[1,16]{1,0:T(1,128)} %bitcast.8, bf16[2,192,256]{2,1,0:T(8,128)(2,1)} %get-tuple-element.7.lines_hbm, f32[16,192,256]{2,1,0:T(8,128)} %get-tuple-element.8.sums_hbm, f32[2,128,256]{2,1,0:T(8,128)} %get-tuple-element.9.residual_hbm), custom_call_target="tpu_custom_call" | custom-call | tf_op jit(solution)/shard_map/pallas_call | solution.py:725
